TPU v7x, 128 devices: a whole 4x4x4 slice. The times are simulated.
128 devices in a mesh: rep: 32 (over z, y, x_hi), tp: 4 (over x_lo, core).
Axes of the slice: x: 4 (x_hi: 2, x_lo: 2; x = x_hi * 2 + x_lo), y: 4, z: 4, core: 2. Of those that a mesh axis runs over, the one named last changes fastest.
Arguments:
- normed_input_rows: bfloat16 [4, 2048, 8192], P(None, 'rep', 'tp'), may hold values from -6 to 6
- queries: bfloat16 [4, 2048, 8192], P(None, 'rep', 'tp'), may hold values from -64 to 64
- key_weight: bfloat16 [8192, 1024], P(None, 'tp'), may hold values from -0.0625 to 0.0625
- value_weight: bfloat16 [8192, 1024], P(None, 'tp'), may hold values from -0.0625 to 0.0625
- cached_key_store: bfloat16 [2048, 256, 1024], P('rep', None, 'tp'), may hold values from -16 to 16
- cached_value_store: bfloat16 [2048, 256, 1024], P('rep', None, 'tp'), may hold values from -6 to 6
- adapter_down_weight: bfloat16 [128, 8192, 256], P('rep', 'tp'), may hold values from -0.0625 to 0.0625
- adapter_up_weight: bfloat16 [128, 2, 128, 1024], P('rep', None, None, 'tp'), may hold values from -0.5 to 0.5
- adapter_index_rows: int32 [4, 2048], P(None, 'rep'), may hold values from 0 to 127, as said below
- adapter_rank_list: int32 [128], P('rep'), may hold values from 16 to 128, as said below
- cache_fill_length: int32 [2048], P('rep'), may hold values from 2 to 256, as said below
Outputs:
- attention_out: bfloat16 [4, 2048, 8192], P(None, 'rep', 'tp')
- new_keys: bfloat16 [4, 2048, 1024], P(None, 'rep', 'tp')
- new_values: bfloat16 [4, 2048, 1024], P(None, 'rep', 'tp')
Inputs may be any that keep to these rules, and one draw needn't show every extreme that they name: `adapter_index_rows`: adapter a is held on index a // 4 of rep. `adapter_rank_list`: A multiple of 16; every index of rep holds an adapter of rank 128. `cache_fill_length`: every index of rep holds a row with 256 filled slots.
All inputs are finite; a program needn't handle non-finite values.
Results may differ from a plain program's by a relative error of at most 0.0054.
Values may be sent and summed in bfloat16 or wider, within the bound.
No kernel may reach another device: no remote copies, remote signals or barrier semaphores. Data moves between devices by JAX's collectives and lax.ppermute only.
A program may use at most 128 MiB of HBM per device.

v0:
```python
import functools
import math

import jax
import jax.numpy as jnp
from jax import lax
from jax.experimental import pallas as pl
from jax.experimental.pallas import tpu as pltpu
from jax.sharding import PartitionSpec as P

HEAD_WIDTH = 128
RANK_PADDED = 128
CAP = 4
LANES = 128

adapter_strength = 16.0
rope_theta = 500000.0
masked_score = -1e30

F32 = jnp.float32
BF16 = jnp.bfloat16
MIB = 1024 * 1024


def cost(flops, moved):
    return pl.CostEstimate(flops=int(flops), bytes_accessed=int(moved), transcendentals=0)


def params(mib, **extra):
    return pltpu.CompilerParams(vmem_limit_bytes=mib * MIB, **extra)


def dispatch_kernel(rows_dev, resident, ids_ref, x_ref, out_ref, sel_ref):
    total = x_ref.shape[0]
    width = x_ref.shape[1]
    slots = out_ref.shape[0]
    per_home = (total // rows_dev) * CAP
    ids = ids_ref[...]
    sub = lax.broadcasted_iota(jnp.int32, (total, total), 0)
    lane = lax.broadcasted_iota(jnp.int32, (total, total), 1)
    ids_r = jnp.concatenate([ids[s : s + 1] for s in range(total // rows_dev)], axis=1)
    diagonal = jnp.where(sub == lane, ids_r.astype(F32), 0.0)
    ids_c = jnp.sum(diagonal, axis=1, keepdims=True).astype(jnp.int32)
    own_r = lax.div(ids_r, resident)
    own_c = lax.div(ids_c, resident)
    same = (own_c == own_r) & (lax.div(sub, rows_dev) == lax.div(lane, rows_dev))
    before_row = jnp.sum(jnp.where(same & (sub < lane), 1.0, 0.0), axis=0, keepdims=True)
    before_col = jnp.sum(jnp.where(same & (lane < sub), 1.0, 0.0), axis=1, keepdims=True)
    step_r = lax.div(lax.broadcasted_iota(jnp.int32, (1, total), 1), rows_dev)
    step_c = lax.div(lax.broadcasted_iota(jnp.int32, (total, 1), 0), rows_dev)
    place_r = own_r * per_home + step_r * CAP + before_row.astype(jnp.int32)
    place_c = own_c * per_home + step_c * CAP + before_col.astype(jnp.int32)
    sel_ref[...] = jnp.where(
        lax.broadcasted_iota(jnp.int32, (total, slots), 1) == place_c, 1.0, 0.0
    ).astype(BF16)
    spread = jnp.where(
        lax.broadcasted_iota(jnp.int32, (slots, total), 0) == place_r, 1.0, 0.0
    ).astype(BF16)
    local = ids_c - own_c * resident
    marks = jnp.where(
        lax.broadcasted_iota(jnp.int32, (total, LANES), 1) == local, 1.0, 0.0
    ).astype(BF16)
    chunk = 512
    for start in range(0, width, chunk):
        out_ref[:, start : start + chunk] = jnp.dot(
            spread, x_ref[:, start : start + chunk], preferred_element_type=F32
        ).astype(BF16)
    out_ref[:, width:] = jnp.dot(spread, marks, preferred_element_type=F32).astype(BF16)


def dispatch(ids, x, rows_dev, resident, replicas):
    total, width = x.shape
    slots = replicas * (total // rows_dev) * CAP
    return pl.pallas_call(
        functools.partial(dispatch_kernel, rows_dev, resident),
        out_shape=(
            jax.ShapeDtypeStruct((slots, width + LANES), BF16),
            jax.ShapeDtypeStruct((total, slots), BF16),
        ),
        compiler_params=params(16),
        cost_estimate=cost(2 * slots * total * width, 2 * (total + slots) * width),
        name="dispatch",
    )(ids, x)


def mark_column(tail, index):
    lane = lax.broadcasted_iota(jnp.int32, tail.shape, 1)
    return jnp.sum(jnp.where(lane == index, tail.astype(F32), 0.0), axis=1, keepdims=True)


def down_kernel(odd_ref, landed_ref, weight_ref, factor_ref, keep_ref, send_ref, sum_ref):
    a = pl.program_id(0)
    width = weight_ref.shape[1]
    half = keep_ref.shape[0]
    product = jnp.dot(landed_ref[:, :width], weight_ref[0], preferred_element_type=F32)
    part = product * (mark_column(landed_ref[:, width:], a) * factor_ref[0])

    @pl.when(a == 0)
    def _():
        sum_ref[...] = part

    @pl.when(a > 0)
    def _():
        sum_ref[...] += part

    @pl.when(a == pl.num_programs(0) - 1)
    def _():
        odd = odd_ref[0] == 1
        low, high = sum_ref[:half], sum_ref[half:]
        keep_ref[...] = jnp.where(odd, high, low)
        send_ref[...] = jnp.where(odd, low, high)


def down(odd, landed, weight, factor):
    slots, wide = landed.shape
    count, width, ranks = weight.shape
    half = jax.ShapeDtypeStruct((slots // 2, ranks), F32)
    kept = pl.BlockSpec((slots // 2, ranks), lambda a, p: (0, 0))
    return pl.pallas_call(
        down_kernel,
        grid_spec=pltpu.PrefetchScalarGridSpec(
            num_scalar_prefetch=1,
            grid=(count,),
            in_specs=[
                pl.BlockSpec((slots, wide), lambda a, p: (0, 0)),
                pl.BlockSpec((1, width, ranks), lambda a, p: (a, 0, 0)),
                pl.BlockSpec((1, 1, ranks), lambda a, p: (a, 0, 0)),
            ],
            out_specs=(kept, kept),
            scratch_shapes=[pltpu.VMEM((slots, ranks), F32)],
        ),
        out_shape=(half, half),
        compiler_params=params(16),
        cost_estimate=cost(2 * count * slots * width * ranks, 2 * (slots * wide + count * width * ranks)),
        name="down",
    )(odd, landed, weight, factor.reshape(count, 1, ranks))


def up_kernel(odd_ref, own_ref, other_ref, tail_ref, weight_ref, out_ref):
    count, _, ranks, columns = weight_ref.shape
    odd = odd_ref[0] == 1
    tail = tail_ref[...]
    marks = [mark_column(tail, a).astype(BF16) for a in range(count)]
    own, other = own_ref[...].astype(F32), other_ref[...].astype(F32)
    whole = jnp.concatenate([jnp.where(odd, other, own), jnp.where(odd, own, other)], axis=0).astype(BF16)
    for u in range(2):
        mid = whole[:, u * ranks : (u + 1) * ranks]
        total = None
        for a in range(count):
            term = jnp.dot(mid * marks[a], weight_ref[a, u], preferred_element_type=F32)
            total = term if total is None else total + term
        out_ref[:, u * columns : (u + 1) * columns] = total.astype(BF16)


def up(odd, own, other, landed, weight):
    slots = landed.shape[0]
    count, _, ranks, columns = weight.shape
    last = landed.shape[1] // LANES - 1
    half = pl.BlockSpec(own.shape, lambda i, p: (0, 0))
    return pl.pallas_call(
        up_kernel,
        grid_spec=pltpu.PrefetchScalarGridSpec(
            num_scalar_prefetch=1,
            grid=(1,),
            in_specs=[
                half,
                half,
                pl.BlockSpec((slots, LANES), lambda i, p: (0, last)),
                pl.BlockSpec(weight.shape, lambda i, p: (0, 0, 0, 0)),
            ],
            out_specs=pl.BlockSpec((slots, 2 * columns), lambda i, p: (0, 0)),
        ),
        out_shape=jax.ShapeDtypeStruct((slots, 2 * columns), BF16),
        compiler_params=params(12),
        cost_estimate=cost(4 * count * slots * ranks * columns, 4 * slots * columns),
        name="up",
    )(odd, own, other, landed, weight)


def base_kernel(first, place_ref, *refs):
    if first:
        x0, x1, kw_ref, vw_ref, out_ref = refs
    else:
        x0, x1, kw_ref, vw_ref, before_ref, out_ref = refs
    j = pl.program_id(0)
    columns = kw_ref.shape[1]
    for index, x_ref in enumerate((x0, x1)):

        @pl.when(j == index)
        def _(index=index, x_ref=x_ref):
            for number, w_ref in enumerate((kw_ref, vw_ref)):
                term = jnp.dot(x_ref[...], w_ref[...], preferred_element_type=F32)
                where = (slice(None), slice(number * columns, (number + 1) * columns))
                if index > 0:
                    out_ref[where] += term
                elif first:
                    out_ref[where] = term
                else:
                    out_ref[where] = before_ref[where] + term


def base(places, shares, key_weight, value_weight, before=None):
    total, width = shares[0].shape
    columns = key_weight.shape[1]
    whole = pl.BlockSpec((total, width), lambda j, p: (0, 0))
    slab = pl.BlockSpec((width, columns), lambda j, p: (p[j], 0))
    result = pl.BlockSpec((total, 2 * columns), lambda j, p: (0, 0))
    more = () if before is None else (before,)
    return pl.pallas_call(
        functools.partial(base_kernel, before is None),
        grid_spec=pltpu.PrefetchScalarGridSpec(
            num_scalar_prefetch=1,
            grid=(2,),
            in_specs=[whole] * 2 + [slab] * 2 + [result] * len(more),
            out_specs=result,
        ),
        out_shape=jax.ShapeDtypeStruct((total, 2 * columns), F32),
        compiler_params=params(20),
        cost_estimate=cost(8 * total * width * columns, 4 * total * width + 8 * width * columns),
        name="base",
    )(places, *shares, key_weight, value_weight, *more)


def stored_kernel(rows, length_ref, q_ref, k_ref, v_ref, out_ref, lse_ref):
    first = pl.program_id(0) * rows
    slots = k_ref.shape[1]
    groups = k_ref.shape[2] // HEAD_WIDTH
    per_group = q_ref.shape[1] // groups
    scale = 1.0 / math.sqrt(HEAD_WIDTH)
    lane = lax.broadcasted_iota(jnp.int32, (per_group, slots), 1)
    pieces = [
        (r, slice(g * per_group, (g + 1) * per_group), slice(g * HEAD_WIDTH, (g + 1) * HEAD_WIDTH))
        for r in range(rows)
        for g in range(groups)
    ]
    raw = [
        lax.dot_general(
            q_ref[r, mine, :], k_ref[r, :, head], (((1,), (1,)), ((), ())), preferred_element_type=F32
        )
        for r, mine, head in pieces
    ]
    shares = []
    for (r, mine, head), scores in zip(pieces, raw):
        scores = jnp.where(lane < length_ref[first + r], scores * scale, masked_score)
        top = jnp.max(scores, axis=1, keepdims=True)
        weights = jnp.exp(scores - top)
        shares.append((weights.astype(BF16), top, jnp.sum(weights, axis=1, keepdims=True)))
    mixed = [
        jnp.dot(weights, v_ref[r, :, head], preferred_element_type=F32)
        for (r, mine, head), (weights, top, norm) in zip(pieces, shares)
    ]
    for (r, mine, head), (weights, top, norm), value in zip(pieces, shares, mixed):
        out_ref[r, mine, :] = value / norm
        lse_ref[r, mine, :] = jnp.broadcast_to(top + jnp.log(norm), (per_group, LANES))


def stored(lengths, q_rows, keys, values):
    count, slots, width = keys.shape
    rows = 8
    queries = q_rows.shape[1]
    block = pl.BlockSpec((rows, queries, HEAD_WIDTH), lambda i, n: (i, 0, 0))
    cache = pl.BlockSpec((rows, slots, width), lambda i, n: (i, 0, 0))
    shape = jax.ShapeDtypeStruct((count, queries, HEAD_WIDTH), F32)
    return pl.pallas_call(
        functools.partial(stored_kernel, rows),
        grid_spec=pltpu.PrefetchScalarGridSpec(
            num_scalar_prefetch=1,
            grid=(count // rows,),
            in_specs=[block, cache, cache],
            out_specs=(block, block),
        ),
        out_shape=(shape, shape),
        compiler_params=params(24),
        cost_estimate=cost(4 * count * queries * slots * HEAD_WIDTH, 4 * count * slots * width),
        name="stored",
    )(lengths, q_rows, keys, values)


def final_kernel(
    delivered_ref, sel_ref, base_ref, cos_ref, sin_ref, q_ref, old_ref, lse_ref, out_ref, key_ref, value_ref
):
    steps, block, wide = base_ref.shape
    rows = steps * block
    columns = wide // 2
    groups = columns // HEAD_WIDTH
    heads = q_ref.shape[2] // columns
    scale = 1.0 / math.sqrt(HEAD_WIDTH)
    sel = sel_ref[...].reshape(rows, sel_ref.shape[2])
    summed = base_ref[...].reshape(rows, wide) + jnp.dot(sel, delivered_ref[...], preferred_element_type=F32)
    cos = cos_ref[...].reshape(rows, HEAD_WIDTH)
    sin = sin_ref[...].reshape(rows, HEAD_WIDTH)
    ones = jnp.ones((rows, LANES), BF16)
    keys, both = [], []
    for g in range(groups):
        head = slice(g * HEAD_WIDTH, (g + 1) * HEAD_WIDTH)
        piece = summed[:, head]
        turned = (piece * cos + pltpu.roll(piece, HEAD_WIDTH // 2, 1) * sin).astype(BF16)
        keys.append(turned)
        key_ref[:, :, head] = turned.reshape(steps, block, HEAD_WIDTH)
        fresh = summed[:, columns + g * HEAD_WIDTH : columns + (g + 1) * HEAD_WIDTH].astype(BF16)
        both.append(jnp.concatenate([fresh, ones], axis=1))
        value_ref[:, :, head] = fresh.reshape(steps, block, HEAD_WIDTH)
    sub = lax.broadcasted_iota(jnp.int32, (heads * block, rows), 0)
    lane = lax.broadcasted_iota(jnp.int32, (heads * block, rows), 1)
    same_row = lax.rem(sub, block) == lax.rem(lane, block)
    of_step = lax.div(lane, block)
    pieces = [(g, t) for g in range(groups) for t in range(steps)]

    def lanes(g, h):
        return slice((g * heads + h) * HEAD_WIDTH, (g * heads + h + 1) * HEAD_WIDTH)

    raw = []
    for g, t in pieces:
        q = jnp.concatenate([q_ref[t, :, lanes(g, h)] for h in range(heads)], axis=0)
        raw.append(lax.dot_general(q, keys[g], (((1,), (1,)), ((), ())), preferred_element_type=F32))
    shares = []
    for (g, t), scores in zip(pieces, raw):
        first = (g * steps + t) * heads
        lse = lse_ref[first : first + heads].reshape(heads * block, LANES)
        scores = jnp.where(same_row & (of_step <= t), scores * scale, masked_score)
        top = jnp.maximum(lse, jnp.max(scores, axis=1, keepdims=True))
        shares.append((jnp.exp(scores - top[:, :1]).astype(BF16), jnp.exp(lse - top)))
    mixed = [jnp.dot(w, both[g], preferred_element_type=F32) for (g, t), (w, kept) in zip(pieces, shares)]
    for (g, t), (w, kept), value in zip(pieces, shares, mixed):
        first = (g * steps + t) * heads
        old = old_ref[first : first + heads].reshape(heads * block, HEAD_WIDTH)
        result = (old * kept + value[:, :HEAD_WIDTH]) / (kept + value[:, HEAD_WIDTH:])
        result = result.astype(BF16)
        for h in range(heads):
            out_ref[t, :, lanes(g, h)] = result[h * block : (h + 1) * block]


def final(delivered, sel, base_rows, cos, sin, queries, old, lse):
    steps, rows_dev, width = queries.shape
    wide = base_rows.shape[1]
    slots = sel.shape[1]
    block = min(rows_dev, LANES // steps)

    def rows_of(last):
        return pl.BlockSpec((steps, block, last), lambda i: (0, i, 0))

    def shaped(array):
        return array.reshape(steps, rows_dev, array.shape[-1])

    stored_part = pl.BlockSpec((old.shape[0], block, LANES), lambda i: (0, i, 0))
    fresh = jax.ShapeDtypeStruct((steps, rows_dev, wide // 2), BF16)
    return pl.pallas_call(
        final_kernel,
        grid=(rows_dev // block,),
        in_specs=[
            pl.BlockSpec(delivered.shape, lambda i: (0, 0)),
            rows_of(slots),
            rows_of(wide),
            rows_of(HEAD_WIDTH),
            rows_of(HEAD_WIDTH),
            rows_of(width),
            stored_part,
            stored_part,
        ],
        out_specs=(rows_of(width), rows_of(wide // 2), rows_of(wide // 2)),
        out_shape=(jax.ShapeDtypeStruct(queries.shape, BF16), fresh, fresh),
        compiler_params=params(24),
        cost_estimate=cost(1e9, 8 * MIB),
        name="final",
    )(delivered, shaped(sel), shaped(base_rows), shaped(cos), shaped(sin), queries, old, lse)


def swap(x, bit):
    count = lax.axis_size("tp")
    return lax.ppermute(x, "tp", [(i, i ^ bit) for i in range(count)])


def per_device(
    normed_input_rows,
    queries,
    key_weight,
    value_weight,
    cached_key_store,
    cached_value_store,
    adapter_down_weight,
    adapter_up_weight,
    adapter_index_rows,
    adapter_rank_list,
    cache_fill_length,
):
    steps, rows_dev, width = normed_input_rows.shape
    total = steps * rows_dev
    replicas = lax.axis_size("rep")
    resident = adapter_down_weight.shape[0]
    columns = key_weight.shape[1]
    groups = columns // HEAD_WIDTH
    heads = queries.shape[2] // columns
    t = lax.axis_index("tp")
    odd = jnp.reshape(t % 2, (1,)).astype(jnp.int32)

    x = normed_input_rows.reshape(total, width)
    outgoing, sel = dispatch(adapter_index_rows, x, rows_dev, resident, replicas)
    landed = lax.all_to_all(outgoing, "rep", split_axis=0, concat_axis=0, tiled=True)

    queries, x_near, outgoing = lax.optimization_barrier((queries, x, outgoing))
    q_rows = queries.reshape(steps, rows_dev, groups, heads, HEAD_WIDTH)
    q_rows = q_rows.transpose(1, 2, 0, 3, 4).reshape(rows_dev, groups * steps * heads, HEAD_WIDTH)
    old, lse = stored(cache_fill_length, q_rows, cached_key_store, cached_value_store)
    old = old.transpose(1, 0, 2)
    lse = lse.transpose(1, 0, 2)

    positions = (
        cache_fill_length[None, :] + jnp.arange(steps, dtype=jnp.int32)[:, None]
    ).reshape(total)
    half = HEAD_WIDTH // 2
    frequency = jnp.power(rope_theta, -(jnp.arange(half, dtype=F32) * (2.0 / HEAD_WIDTH)))
    angles = positions.astype(F32)[:, None] * frequency[None, :]
    cos, sin = jnp.cos(angles), jnp.sin(angles)
    cos = jnp.concatenate([cos, cos], axis=1)
    sin = jnp.concatenate([-sin, sin], axis=1)

    slot = jnp.arange(2 * RANK_PADDED, dtype=jnp.int32) % RANK_PADDED
    factor = jnp.where(
        slot[None, :] < adapter_rank_list[:, None],
        adapter_strength / adapter_rank_list.astype(F32)[:, None],
        0.0,
    )

    near = swap(x_near, 1)
    base_rows = base(jnp.stack([t, t ^ 1]).astype(jnp.int32), (x, near), key_weight, value_weight)
    landed, old, lse, cos, sin, base_rows, factor = lax.optimization_barrier(
        (landed, old, lse, cos, sin, base_rows, factor)
    )

    keep, send = down(odd, landed, adapter_down_weight, factor)
    part = keep + swap(send, 1)
    arrived = swap(part.astype(BF16), 2)
    x_far, arrived = lax.optimization_barrier((x, arrived))
    far = swap(x_far, 2)
    own = (part + arrived.astype(F32)).astype(BF16)
    other = swap(own, 1)
    returned = up(odd, own, other, landed, adapter_up_weight)
    delivered = lax.all_to_all(returned, "rep", split_axis=0, concat_axis=0, tiled=True)
    far, _ = lax.optimization_barrier((far, returned))
    far_near = swap(far, 1)
    base_rows = base(
        jnp.stack([t ^ 2, t ^ 3]).astype(jnp.int32), (far, far_near), key_weight, value_weight, base_rows
    )
    return final(delivered, sel, base_rows, cos, sin, queries, old, lse)


def solution(mesh):
    return jax.shard_map(
        per_device,
        mesh=mesh,
        in_specs=(
            P(None, "rep", "tp"),
            P(None, "rep", "tp"),
            P(None, "tp"),
            P(None, "tp"),
            P("rep", None, "tp"),
            P("rep", None, "tp"),
            P("rep", "tp", None),
            P("rep", None, None, "tp"),
            P(None, "rep"),
            P("rep"),
            P("rep"),
        ),
        out_specs=(P(None, "rep", "tp"), P(None, "rep", "tp"), P(None, "rep", "tp")),
        check_vma=False,
    )
```

profile of v0, /device:TPU:1, one launch (start us, length us, event | category | flops | bytes accessed | tf_op | source)
XLA Modules:
  0.0 114.3 jit_solution(9453436206744834928)
XLA Ops:
  3.6 1.4 %copy-done.10 = bf16[512,2176]{1,0:T(8,128)(2,1)} copy-done((bf16[512,2176]{1,0:T(8,128)(2,1)}, bf16[512,2176]{1,0:T(8,128)(2,1)S(1)}, u32[]{:S(2)}) %copy-start.10) | copy-done | bytes 2228248
  5.7 11.5 %all-to-all-start = ((bf16[32,16,2176]{2,1,0:T(8,128)(2,1)}), bf16[32,16,2176]{2,1,0:T(8,128)(2,1)S(1)}, u32[]{:S(2)}, u32[]{:S(2)}) async-start(bf16[32,16,2176]{2,1,0:T(8,128)(2,1)} %bitcast.29), calls=%async_computation | async-start | bytes 4456448 | tf_op jit(solution)/shard_map/all_to_all | solution.py:398
  19.6 3.4 %copy-done.4 = bf16[64,256,256]{2,1,0:T(8,128)(2,1)S(1)} copy-done((bf16[64,256,256]{2,1,0:T(8,128)(2,1)S(1)}, bf16[64,256,256]{2,1,0:T(8,128)(2,1)}, u32[]{:S(2)}) %copy-start.4) | copy-done | bytes 8388632
  23.0 3.4 %copy-done.5 = bf16[64,256,256]{2,1,0:T(8,128)(2,1)S(1)} copy-done((bf16[64,256,256]{2,1,0:T(8,128)(2,1)S(1)}, bf16[64,256,256]{2,1,0:T(8,128)(2,1)}, u32[]{:S(2)}) %copy-start.5) | copy-done | bytes 8388632
  26.4 6.3 %stored.1 = (f32[64,64,128]{2,1,0:T(8,128)S(1)}, f32[64,64,128]{2,1,0:T(8,128)S(1)}) custom-call(s32[64]{0:T(128)S(1)} %copy-done.25, bf16[64,64,128]{2,1,0:T(8,128)(2,1)S(1)} %bitcast.27, bf16[64,256,256]{2,1,0:T(8,128)(2,1)S(1)} %copy-done.4, bf16[64,256,256]{2,1,0:T(8,128)(2,1)S(1)} %copy-done.5), custom_call_target="tpu_custom_call" | custom-call | flops 536870912 | bytes 16777216 | tf_op jit(solution)/shard_map/stored/pallas_call | solution.py:264
  32.9 4.5 %copy_bitcast_fusion = (f32[64,64,128]{2,1,0:T(8,128)}, f32[64,64,128]{2,1,0:T(8,128)}) fusion(f32[64,64,128]{2,1,0:T(8,128)S(1)} %get-tuple-element.24, f32[64,64,128]{2,1,0:T(8,128)S(1)} %get-tuple-element.23), kind=kLoop, calls=%fused_computation | loop fusion | bytes 8388608 | tf_op jit(solution)/shard_map/transpose | solution.py:405
  37.4 3.2 %base.2.refs_4_ = f32[256,512]{1,0:T(8,128)S(1)} custom-call(s32[2]{0:T(128)S(1)} %pad_add_fusion.place_ref, bf16[256,2048]{1,0:T(8,128)(2,1)S(1)} %bitcast.33, bf16[256,2048]{1,0:T(8,128)(2,1)} %collective-permute-done.refs_1_, bf16[8192,256]{1,0:T(8,128)(2,1)S(1)} %copy-done, bf16[8192,256]{1,0:T(8,128)(2,1)S(1)} %copy-done.2), custom_call_target="tpu_custom_call" | custom-call | flops 1073741824 | bytes 6291456 | tf_op jit(solution)/shard_map/base/pallas_call | solution.py:209
  41.5 6.5 %all-to-all-done = bf16[32,16,2176]{2,1,0:T(8,128)(2,1)S(1)} async-done(((bf16[32,16,2176]{2,1,0:T(8,128)(2,1)}), bf16[32,16,2176]{2,1,0:T(8,128)(2,1)S(1)}, u32[]{:S(2)}, u32[]{:S(2)}) %all-to-all-start) | async-done | bytes 2228256 | tf_op jit(solution)/shard_map/all_to_all | solution.py:398
  48.0 2.2 %copy-done.26 = bf16[4,2048,256]{2,1,0:T(8,128)(2,1)S(1)} copy-done((bf16[4,2048,256]{2,1,0:T(8,128)(2,1)S(1)}, bf16[4,2048,256]{2,1,0:T(8,128)(2,1)}, u32[]{:S(2)}) %copy-start.26) | copy-done | bytes 4194328
  50.2 3.1 %down.1 = (f32[256,256]{1,0:T(8,128)S(1)}, f32[256,256]{1,0:T(8,128)S(1)}) custom-call(s32[1]{0:T(128)} %bitcast.odd_ref, bf16[512,2176]{1,0:T(8,128)(2,1)S(1)} %bitcast.25, bf16[4,2048,256]{2,1,0:T(8,128)(2,1)S(1)} %copy-done.26, f32[4,1,256]{2,1,0:T(1,128)S(1)} %reshape.75.factor_ref), custom_call_target="tpu_custom_call" | custom-call | flops 2147483648 | bytes 6422528 | tf_op jit(solution)/shard_map/down/pallas_call | solution.py:119
  53.3 2.2 %collective-permute-start.1 = (f32[256,256]{1,0:T(8,128)S(1)}, f32[256,256]{1,0:T(8,128)S(1)}, u32[]{:S(2)}, u32[]{:S(2)}) collective-permute-start(f32[256,256]{1,0:T(8,128)S(1)} %get-tuple-element.29), channel_id=1, source_target_pairs={{0,1},{1,0},{2,3},{3,2},{4,5},{5,4},{6,7},{7,6},{8,9},{9,8},{10,11... | collective-permute-start | bytes 786440 | tf_op jit(solution)/shard_map/ppermute | solution.py:370
  57.2 4.3 %collective-permute-done.2 = bf16[256,256]{1,0:T(8,128)(2,1)S(1)} collective-permute-done((bf16[256,256]{1,0:T(8,128)(2,1)S(1)}, bf16[256,256]{1,0:T(8,128)(2,1)S(1)}, u32[]{:S(2)}, u32[]{:S(2)}) %collective-permute-start.2) | collective-permute-done | bytes 131104 | tf_op jit(solution)/shard_map/ppermute | solution.py:370
  62.0 1.6 %collective-permute-start.3 = (bf16[256,256]{1,0:T(8,128)(2,1)S(1)}, bf16[256,256]{1,0:T(8,128)(2,1)S(1)}, u32[]{:S(2)}, u32[]{:S(2)}) collective-permute-start(bf16[256,256]{1,0:T(8,128)(2,1)S(1)} %add_convert_fusion.own_ref), channel_id=1, source_target_pairs={{0,1},{1,0},{2,3},{3,2},{4,5},{5,4},{6,7},{7,6},{8,9},{9,8},{10,11... | collective-permute-start | bytes 393224 | tf_op jit(solution)/shard_map/ppermute | solution.py:370
  64.5 1.6 %up.1 = bf16[512,512]{1,0:T(8,128)(2,1)} custom-call(s32[1]{0:T(128)} %bitcast.odd_ref, bf16[256,256]{1,0:T(8,128)(2,1)S(1)} %add_convert_fusion.own_ref, bf16[256,256]{1,0:T(8,128)(2,1)S(1)} %collective-permute-done.3.other_ref, bf16[512,2176]{1,0:T(8,128)(2,1)S(1)} %bitcast.26, bf16[4,2,128,256]{3,2,1,0:T(8,128)(2,1)S(1)} %copy-done.22), custom_call_target="tpu_custom_call" | custom-call | flops 268435456 | bytes 524288 | tf_op jit(solution)/shard_map/up/pallas_call | solution.py:160
  66.1 18.9 %collective-permute-done.4.refs_0_ = bf16[256,2048]{1,0:T(8,128)(2,1)S(1)} collective-permute-done((bf16[256,2048]{1,0:T(8,128)(2,1)S(1)}, bf16[256,2048]{1,0:T(8,128)(2,1)S(1)}, u32[]{:S(2)}, u32[]{:S(2)}) %collective-permute-start.4) | collective-permute-done | bytes 1048608 | tf_op jit(solution)/shard_map/ppermute | solution.py:370
  85.0 2.1 %collective-permute-start.5 = (bf16[256,2048]{1,0:T(8,128)(2,1)S(1)}, bf16[256,2048]{1,0:T(8,128)(2,1)S(1)}, u32[]{:S(2)}, u32[]{:S(2)}) collective-permute-start(bf16[256,2048]{1,0:T(8,128)(2,1)S(1)} %collective-permute-done.4.refs_0_), channel_id=1, source_target_pairs={{0,1},{1,0},{2,3},{3,2},{4,5},{5,4},{6,7},{7,6},{8,9},{9,8},{10,11... | collective-permute-start | bytes 3145736 | tf_op jit(solution)/shard_map/ppermute | solution.py:370
  87.1 5.2 %all-to-all-start.1 = ((bf16[32,16,512]{2,1,0:T(8,128)(2,1)}), bf16[32,16,512]{2,1,0:T(8,128)(2,1)}, u32[]{:S(2)}, u32[]{:S(2)}) async-start(bf16[32,16,512]{2,1,0:T(8,128)(2,1)} %bitcast.10), calls=%async_computation.1 | async-start | bytes 1048576 | tf_op jit(solution)/shard_map/all_to_all | solution.py:438
  93.4 2.2 %copy-done.1 = bf16[8192,256]{1,0:T(8,128)(2,1)S(1)} copy-done((bf16[8192,256]{1,0:T(8,128)(2,1)S(1)}, bf16[8192,256]{1,0:T(8,128)(2,1)}, u32[]{:S(2)}) %copy-start.1) | copy-done | bytes 4194328
  95.5 2.2 %copy-done.3 = bf16[8192,256]{1,0:T(8,128)(2,1)S(1)} copy-done((bf16[8192,256]{1,0:T(8,128)(2,1)S(1)}, bf16[8192,256]{1,0:T(8,128)(2,1)}, u32[]{:S(2)}) %copy-start.3) | copy-done | bytes 4194328
  98.8 1.2 %copy-done.16 = bf16[256,2048]{1,0:T(8,128)(2,1)S(1)} copy-done((bf16[256,2048]{1,0:T(8,128)(2,1)S(1)}, bf16[256,2048]{1,0:T(8,128)(2,1)}, u32[]{:S(2)}) %copy-start.16) | copy-done | bytes 1048600
  101.2 2.0 %base.3 = f32[256,512]{1,0:T(8,128)S(1)} custom-call(s32[2]{0:T(128)S(1)} %pad_add_fusion.1.place_ref, bf16[256,2048]{1,0:T(8,128)(2,1)S(1)} %copy-done.16, bf16[256,2048]{1,0:T(8,128)(2,1)S(1)} %copy-done.18, bf16[8192,256]{1,0:T(8,128)(2,1)S(1)} %copy-done.1, bf16[8192,256]{1,0:T(8,128)(2,1)S(1)} %copy-done.3, f32[256,512]{1,0:T(8,128)S(1)} %copy-done.12), custom_call_target="tpu_custom_call" | custom-call | flops 1073741824 | bytes 6291456 | tf_op jit(solution)/shard_map/base/pallas_call | solution.py:209
  104.0 1.3 %all-to-all-done.1 = bf16[32,16,512]{2,1,0:T(8,128)(2,1)} async-done(((bf16[32,16,512]{2,1,0:T(8,128)(2,1)}), bf16[32,16,512]{2,1,0:T(8,128)(2,1)}, u32[]{:S(2)}, u32[]{:S(2)}) %all-to-all-start.1) | async-done | bytes 524320 | tf_op jit(solution)/shard_map/all_to_all | solution.py:438
  105.4 1.6 %copy-done.7 = f32[64,64,128]{2,1,0:T(8,128)S(1)} copy-done((f32[64,64,128]{2,1,0:T(8,128)S(1)}, f32[64,64,128]{2,1,0:T(8,128)}, u32[]{:S(2)}) %copy-start.7) | copy-done | bytes 2097176
  108.9 5.4 %final.1 = (bf16[4,64,2048]{2,1,0:T(8,128)(2,1)}, bf16[4,64,256]{2,1,0:T(8,128)(2,1)}, bf16[4,64,256]{2,1,0:T(8,128)(2,1)}) custom-call(bf16[512,512]{1,0:T(8,128)(2,1)} %bitcast.11.delivered_ref, bf16[4,64,512]{2,1,0:T(8,128)(2,1)S(1)} %bitcast.37, f32[4,64,512]{2,1,0:T(8,128)S(1)} %bitcast.30, f32[4,64,128]{2,1,0:T(8,128)S(1)} %bitcast.35, ...), custom_call_target="tpu_custom_call" | custom-call | flops 1000000000 | bytes 8388608 | tf_op jit(solution)/shard_map/final/pallas_call | solution.py:347
  (73 shorter events, 16.4 us)
Async XLA Ops:
  5.7 12.5 %copy-start.8 = (bf16[4,64,2048]{2,1,0:T(8,128)(2,1)S(1)}, bf16[4,64,2048]{2,1,0:T(8,128)(2,1)}, u32[]{:S(2)}) copy-start(bf16[4,64,2048]{2,1,0:T(8,128)(2,1)} %q_ref) | copy-start | bytes 3145732
  5.7 42.3 %all-to-all-start = ((bf16[32,16,2176]{2,1,0:T(8,128)(2,1)}), bf16[32,16,2176]{2,1,0:T(8,128)(2,1)S(1)}, u32[]{:S(2)}, u32[]{:S(2)}) async-start(bf16[32,16,2176]{2,1,0:T(8,128)(2,1)} %bitcast.29), calls=%async_computation | async-start | bytes 4456448 | tf_op jit(solution)/shard_map/all_to_all | solution.py:398
  17.2 20.2 %collective-permute-start = (bf16[256,2048]{1,0:T(8,128)(2,1)}, bf16[256,2048]{1,0:T(8,128)(2,1)}, u32[]{:S(2)}, u32[]{:S(2)}) collective-permute-start(bf16[256,2048]{1,0:T(8,128)(2,1)} %bitcast.31), channel_id=1, source_target_pairs={{0,1},{1,0},{2,3},{3,2},{4,5},{5,4},{6,7},{7,6},{8,9},{9,8},{10,11... | collective-permute-start | bytes 3145736 | tf_op jit(solution)/shard_map/ppermute | solution.py:370
  19.6 3.4 %copy-start.4 = (bf16[64,256,256]{2,1,0:T(8,128)(2,1)S(1)}, bf16[64,256,256]{2,1,0:T(8,128)(2,1)}, u32[]{:S(2)}) copy-start(bf16[64,256,256]{2,1,0:T(8,128)(2,1)} %k_ref.1) | copy-start | bytes 25165828
  23.0 3.4 %copy-start.5 = (bf16[64,256,256]{2,1,0:T(8,128)(2,1)S(1)}, bf16[64,256,256]{2,1,0:T(8,128)(2,1)}, u32[]{:S(2)}) copy-start(bf16[64,256,256]{2,1,0:T(8,128)(2,1)} %v_ref.1) | copy-start | bytes 25165828
  26.4 6.4 %copy-start.28 = (s32[4]{0:T(128)S(1)}, s32[4]{0:T(128)}, u32[]{:S(2)}) copy-start(s32[4]{0:T(128)} %param.20) | copy-start | bytes 52
  26.4 11.0 %copy-start.20 = (bf16[4,64,2048]{2,1,0:T(8,128)(2,1)S(1)}, bf16[4,64,2048]{2,1,0:T(8,128)(2,1)}, u32[]{:S(2)}) copy-start(bf16[4,64,2048]{2,1,0:T(8,128)(2,1)} %param.11) | copy-start | bytes 3145732
  32.9 4.5 %copy-start = (bf16[8192,256]{1,0:T(8,128)(2,1)S(1)}, bf16[8192,256]{1,0:T(8,128)(2,1)}, u32[]{:S(2)}) copy-start(bf16[8192,256]{1,0:T(8,128)(2,1)} %refs_2_.3) | copy-start | bytes 12582916
  32.9 4.5 %copy-start.2 = (bf16[8192,256]{1,0:T(8,128)(2,1)S(1)}, bf16[8192,256]{1,0:T(8,128)(2,1)}, u32[]{:S(2)}) copy-start(bf16[8192,256]{1,0:T(8,128)(2,1)} %refs_3_.3) | copy-start | bytes 12582916
  48.0 2.2 %copy-start.26 = (bf16[4,2048,256]{2,1,0:T(8,128)(2,1)S(1)}, bf16[4,2048,256]{2,1,0:T(8,128)(2,1)}, u32[]{:S(2)}) copy-start(bf16[4,2048,256]{2,1,0:T(8,128)(2,1)} %weight_ref.2) | copy-start | bytes 12582916
  50.2 11.3 %copy-start.21 = (bf16[4,64,2048]{2,1,0:T(8,128)(2,1)S(1)}, bf16[4,64,2048]{2,1,0:T(8,128)(2,1)}, u32[]{:S(2)}) copy-start(bf16[4,64,2048]{2,1,0:T(8,128)(2,1)} %param.11) | copy-start | bytes 3145732
  50.2 14.3 %copy-start.22 = (bf16[4,2,128,256]{3,2,1,0:T(8,128)(2,1)S(1)}, bf16[4,2,128,256]{3,2,1,0:T(8,128)(2,1)}, u32[]{:S(2)}) copy-start(bf16[4,2,128,256]{3,2,1,0:T(8,128)(2,1)} %weight_ref.3) | copy-start | bytes 1572868
  53.3 3.4 %collective-permute-start.1 = (f32[256,256]{1,0:T(8,128)S(1)}, f32[256,256]{1,0:T(8,128)S(1)}, u32[]{:S(2)}, u32[]{:S(2)}) collective-permute-start(f32[256,256]{1,0:T(8,128)S(1)} %get-tuple-element.29), channel_id=1, source_target_pairs={{0,1},{1,0},{2,3},{3,2},{4,5},{5,4},{6,7},{7,6},{8,9},{9,8},{10,11... | collective-permute-start | bytes 786440 | tf_op jit(solution)/shard_map/ppermute | solution.py:370
  56.7 4.8 %collective-permute-start.2 = (bf16[256,256]{1,0:T(8,128)(2,1)S(1)}, bf16[256,256]{1,0:T(8,128)(2,1)S(1)}, u32[]{:S(2)}, u32[]{:S(2)}) collective-permute-start(bf16[256,256]{1,0:T(8,128)(2,1)S(1)} %get-tuple-element.39), channel_id=1, source_target_pairs={{0,2},{1,3},{2,0},{3,1},{4,6},{5,7},{6,4},{7,5},{8,10},{9,11},{10,... | collective-permute-start | bytes 393224 | tf_op jit(solution)/shard_map/ppermute | solution.py:370
  61.5 23.5 %collective-permute-start.4 = (bf16[256,2048]{1,0:T(8,128)(2,1)S(1)}, bf16[256,2048]{1,0:T(8,128)(2,1)S(1)}, u32[]{:S(2)}, u32[]{:S(2)}) collective-permute-start(bf16[256,2048]{1,0:T(8,128)(2,1)S(1)} %bitcast.34), channel_id=1, source_target_pairs={{0,2},{1,3},{2,0},{3,1},{4,6},{5,7},{6,4},{7,5},{8,10},{9,11},{10,... | collective-permute-start | bytes 3145736 | tf_op jit(solution)/shard_map/ppermute | solution.py:370
  62.0 2.5 %collective-permute-start.3 = (bf16[256,256]{1,0:T(8,128)(2,1)S(1)}, bf16[256,256]{1,0:T(8,128)(2,1)S(1)}, u32[]{:S(2)}, u32[]{:S(2)}) collective-permute-start(bf16[256,256]{1,0:T(8,128)(2,1)S(1)} %add_convert_fusion.own_ref), channel_id=1, source_target_pairs={{0,1},{1,0},{2,3},{3,2},{4,5},{5,4},{6,7},{7,6},{8,9},{9,8},{10,11... | collective-permute-start | bytes 393224 | tf_op jit(solution)/shard_map/ppermute | solution.py:370
  85.0 7.4 %copy-start.15 = (bf16[256,2048]{1,0:T(8,128)(2,1)}, bf16[256,2048]{1,0:T(8,128)(2,1)S(1)}, u32[]{:S(2)}) copy-start(bf16[256,2048]{1,0:T(8,128)(2,1)S(1)} %collective-permute-done.4.refs_0_) | copy-start | bytes 3145732
  85.0 7.4 %collective-permute-start.5 = (bf16[256,2048]{1,0:T(8,128)(2,1)S(1)}, bf16[256,2048]{1,0:T(8,128)(2,1)S(1)}, u32[]{:S(2)}, u32[]{:S(2)}) collective-permute-start(bf16[256,2048]{1,0:T(8,128)(2,1)S(1)} %collective-permute-done.4.refs_0_), channel_id=1, source_target_pairs={{0,1},{1,0},{2,3},{3,2},{4,5},{5,4},{6,7},{7,6},{8,9},{9,8},{10,11... | collective-permute-start | bytes 3145736 | tf_op jit(solution)/shard_map/ppermute | solution.py:370
  87.1 18.2 %all-to-all-start.1 = ((bf16[32,16,512]{2,1,0:T(8,128)(2,1)}), bf16[32,16,512]{2,1,0:T(8,128)(2,1)}, u32[]{:S(2)}, u32[]{:S(2)}) async-start(bf16[32,16,512]{2,1,0:T(8,128)(2,1)} %bitcast.10), calls=%async_computation.1 | async-start | bytes 1048576 | tf_op jit(solution)/shard_map/all_to_all | solution.py:438
  93.4 2.2 %copy-start.1 = (bf16[8192,256]{1,0:T(8,128)(2,1)S(1)}, bf16[8192,256]{1,0:T(8,128)(2,1)}, u32[]{:S(2)}) copy-start(bf16[8192,256]{1,0:T(8,128)(2,1)} %refs_2_.3) | copy-start | bytes 12582916
  95.5 2.2 %copy-start.3 = (bf16[8192,256]{1,0:T(8,128)(2,1)S(1)}, bf16[8192,256]{1,0:T(8,128)(2,1)}, u32[]{:S(2)}) copy-start(bf16[8192,256]{1,0:T(8,128)(2,1)} %refs_3_.3) | copy-start | bytes 12582916
  101.2 4.1 %copy-start.6 = (f32[64,64,128]{2,1,0:T(8,128)S(1)}, f32[64,64,128]{2,1,0:T(8,128)}, u32[]{:S(2)}) copy-start(f32[64,64,128]{2,1,0:T(8,128)} %get-tuple-element.38.lse_ref) | copy-start | bytes 6291460
  101.2 4.1 %copy-start.9 = (bf16[4,64,2048]{2,1,0:T(8,128)(2,1)S(1)}, bf16[4,64,2048]{2,1,0:T(8,128)(2,1)}, u32[]{:S(2)}) copy-start(bf16[4,64,2048]{2,1,0:T(8,128)(2,1)} %q_ref) | copy-start | bytes 3145732
  105.4 1.6 %copy-start.7 = (f32[64,64,128]{2,1,0:T(8,128)S(1)}, f32[64,64,128]{2,1,0:T(8,128)}, u32[]{:S(2)}) copy-start(f32[64,64,128]{2,1,0:T(8,128)} %get-tuple-element.37.old_ref) | copy-start | bytes 6291460
  (13 other events, 12.8 us)
where the time goes:
time: 115 us; the launch traced here: 114 us
  waiting for transfers between devices  33.2 us (29%)
  local copies, waits for them, and re-layouts  32.2 us (28%)
  starting transfers between devices  24.5 us (21%)
  Pallas kernels  22.6 us (20%)
    unnamed x59, local copies, waits for them, and re-layouts  27.4 us
    ppermute x6, waiting for transfers between devices, swap(): return lax.ppermute(x, 'tp', [(i, i ^ bit) for i in range(count)])  25.3 us
    all_to_all x1, starting transfers between devices, per_device(): lax.all_to_all(outgoing, 'rep', split_axis=0, concat_axis=0, tiled=True)  11.5 us
    ppermute x6, starting transfers between devices, swap(): return lax.ppermute(x, 'tp', [(i, i ^ bit) for i in range(count)])  7.86 us
    all_to_all x1, waiting for transfers between devices, per_device(): lax.all_to_all(outgoing, 'rep', split_axis=0, concat_axis=0, tiled=True)  6.54 us
    pallas_call x1, Pallas kernels, stored(): pl.pallas_call(functools.partial(stored_kernel, rows), grid_spec=pltpu.Pr...  6.25 us
    pallas_call x1, Pallas kernels, final(): pl.pallas_call(final_kernel, grid=(rows_dev // block,), in_specs=[pl.Bloc...  5.4 us
    pallas_call x2, Pallas kernels, base(): pl.pallas_call(functools.partial(base_kernel, before is None), grid_spec=...  5.23 us
  transfers between devices with their start and end apart: 8, of which 6 were waited for; matrix products, arithmetic and copies ran while one was open for 5% of the time, Pallas kernels for 11%

commit v1 on v0

--- a/solution.py
+++ b/solution.py
@@ -30,11 +30,25 @@
     return pltpu.CompilerParams(vmem_limit_bytes=mib * MIB, **extra)
 
 
-def dispatch_kernel(rows_dev, resident, ids_ref, x_ref, out_ref, sel_ref):
+def dispatch_kernel(
+    rows_dev, resident, ids_hbm, x_hbm, out_hbm, sel_hbm, ids_ref, x_ref, out_ref, sel_ref, in_sem, out_sem
+):
     total = x_ref.shape[0]
     width = x_ref.shape[1]
     slots = out_ref.shape[0]
     per_home = (total // rows_dev) * CAP
+    chunk = 512
+    places = [slice(start, start + chunk) for start in range(0, width, chunk)]
+    count = len(places)
+    fetch_ids = pltpu.make_async_copy(ids_hbm, ids_ref, in_sem.at[count])
+    fetch_ids.start()
+    fetches = [
+        pltpu.make_async_copy(x_hbm.at[:, where], x_ref.at[:, where], in_sem.at[i])
+        for i, where in enumerate(places)
+    ]
+    for fetch in fetches:
+        fetch.start()
+    fetch_ids.wait()
     ids = ids_ref[...]
     sub = lax.broadcasted_iota(jnp.int32, (total, total), 0)
     lane = lax.broadcasted_iota(jnp.int32, (total, total), 1)
@@ -60,24 +74,44 @@
     marks = jnp.where(
         lax.broadcasted_iota(jnp.int32, (total, LANES), 1) == local, 1.0, 0.0
     ).astype(BF16)
-    chunk = 512
-    for start in range(0, width, chunk):
-        out_ref[:, start : start + chunk] = jnp.dot(
-            spread, x_ref[:, start : start + chunk], preferred_element_type=F32
-        ).astype(BF16)
-    out_ref[:, width:] = jnp.dot(spread, marks, preferred_element_type=F32).astype(BF16)
+    sends = [pltpu.make_async_copy(sel_ref, sel_hbm, out_sem.at[count])]
+    sends[0].start()
+    last = slice(width, width + LANES)
+    out_ref[:, last] = jnp.dot(spread, marks, preferred_element_type=F32).astype(BF16)
+    sends.append(pltpu.make_async_copy(out_ref.at[:, last], out_hbm.at[:, last], out_sem.at[count + 1]))
+    sends[1].start()
+    for i, where in enumerate(places):
+        fetches[i].wait()
+        out_ref[:, where] = jnp.dot(spread, x_ref[:, where], preferred_element_type=F32).astype(BF16)
+        send = pltpu.make_async_copy(out_ref.at[:, where], out_hbm.at[:, where], out_sem.at[i])
+        send.start()
+        sends.append(send)
+    for send in sends:
+        send.wait()
+
+
+def in_hbm(count):
+    return [pl.BlockSpec(memory_space=pltpu.HBM)] * count
 
 
 def dispatch(ids, x, rows_dev, resident, replicas):
     total, width = x.shape
     slots = replicas * (total // rows_dev) * CAP
+    outgoing, sel = (slots, width + LANES), (total, slots)
     return pl.pallas_call(
         functools.partial(dispatch_kernel, rows_dev, resident),
-        out_shape=(
-            jax.ShapeDtypeStruct((slots, width + LANES), BF16),
-            jax.ShapeDtypeStruct((total, slots), BF16),
-        ),
-        compiler_params=params(16),
+        in_specs=in_hbm(2),
+        out_specs=tuple(in_hbm(2)),
+        out_shape=(jax.ShapeDtypeStruct(outgoing, BF16), jax.ShapeDtypeStruct(sel, BF16)),
+        scratch_shapes=[
+            pltpu.VMEM(ids.shape, jnp.int32),
+            pltpu.VMEM(x.shape, BF16),
+            pltpu.VMEM(outgoing, BF16),
+            pltpu.VMEM(sel, BF16),
+            pltpu.SemaphoreType.DMA((width // 512 + 1,)),
+            pltpu.SemaphoreType.DMA((width // 512 + 2,)),
+        ],
+        compiler_params=params(60),
         cost_estimate=cost(2 * slots * total * width, 2 * (total + slots) * width),
         name="dispatch",
     )(ids, x)
@@ -171,52 +205,85 @@
             out_specs=pl.BlockSpec((slots, 2 * columns), lambda i, p: (0, 0)),
         ),
         out_shape=jax.ShapeDtypeStruct((slots, 2 * columns), BF16),
-        compiler_params=params(12),
+        compiler_params=params(16),
         cost_estimate=cost(4 * count * slots * ranks * columns, 4 * slots * columns),
         name="up",
     )(odd, own, other, landed, weight)
 
 
-def base_kernel(first, place_ref, *refs):
-    if first:
-        x0, x1, kw_ref, vw_ref, out_ref = refs
-    else:
-        x0, x1, kw_ref, vw_ref, before_ref, out_ref = refs
-    j = pl.program_id(0)
-    columns = kw_ref.shape[1]
-    for index, x_ref in enumerate((x0, x1)):
-
-        @pl.when(j == index)
-        def _(index=index, x_ref=x_ref):
-            for number, w_ref in enumerate((kw_ref, vw_ref)):
-                term = jnp.dot(x_ref[...], w_ref[...], preferred_element_type=F32)
-                where = (slice(None), slice(number * columns, (number + 1) * columns))
-                if index > 0:
-                    out_ref[where] += term
-                elif first:
-                    out_ref[where] = term
-                else:
-                    out_ref[where] = before_ref[where] + term
+def share_copies(place_ref, shares, key_hbm, value_hbm, share_refs, weight_refs, sem):
+    copies = []
+    for i, (share, x_ref, w_ref) in enumerate(zip(shares, share_refs, weight_refs)):
+        unit = x_ref.shape[1]
+        rows = pl.ds(pl.multiple_of(place_ref[i], LANES), unit)
+        copies.append(
+            [
+                pltpu.make_async_copy(share, x_ref, sem.at[i, 0]),
+                pltpu.make_async_copy(key_hbm.at[rows, :], w_ref.at[0], sem.at[i, 1]),
+                pltpu.make_async_copy(value_hbm.at[rows, :], w_ref.at[1], sem.at[i, 2]),
+            ]
+        )
+    return copies
+
+
+def share_scratch(shares, columns):
+    return (
+        [pltpu.VMEM(x.shape, BF16) for x in shares]
+        + [pltpu.VMEM((2, x.shape[1], columns), BF16) for x in shares]
+        + [pltpu.SemaphoreType.DMA((max(1, len(shares)), 3))]
+    )
+
+
+def base_kernel(count, more, place_ref, *refs):
+    shares, refs = refs[:count], refs[count:]
+    key_hbm, value_hbm = refs[:2]
+    before = refs[2] if more else None
+    refs = refs[3:] if more else refs[2:]
+    out_hbm, refs = refs[0], refs[1:]
+    share_refs, weight_refs, sem = refs[:count], refs[count : 2 * count], refs[2 * count]
+    out_ref, out_sem = refs[2 * count + 1 :]
+    copies = share_copies(place_ref, shares, key_hbm, value_hbm, share_refs, weight_refs, sem)
+    for group in copies:
+        for copy in group:
+            copy.start()
+    if more:
+        load = pltpu.make_async_copy(before, out_ref, out_sem.at[2])
+        load.start()
+    columns = key_hbm.shape[1]
+    totals = [None, None]
+    for i in range(count):
+        copies[i][0].wait()
+        for number in range(2):
+            copies[i][1 + number].wait()
+            term = jnp.dot(share_refs[i][...], weight_refs[i][number], preferred_element_type=F32)
+            totals[number] = term if i == 0 else totals[number] + term
+    if more:
+        load.wait()
+    stores = []
+    for number in range(2):
+        where = slice(number * columns, (number + 1) * columns)
+        out_ref[:, where] = totals[number] + out_ref[:, where] if more else totals[number]
+        store = pltpu.make_async_copy(out_ref.at[:, where], out_hbm.at[:, where], out_sem.at[number])
+        store.start()
+        stores.append(store)
+    for store in stores:
+        store.wait()
 
 
 def base(places, shares, key_weight, value_weight, before=None):
-    total, width = shares[0].shape
+    total = shares[0].shape[0]
+    count = len(shares)
     columns = key_weight.shape[1]
-    whole = pl.BlockSpec((total, width), lambda j, p: (0, 0))
-    slab = pl.BlockSpec((width, columns), lambda j, p: (p[j], 0))
-    result = pl.BlockSpec((total, 2 * columns), lambda j, p: (0, 0))
     more = () if before is None else (before,)
     return pl.pallas_call(
-        functools.partial(base_kernel, before is None),
-        grid_spec=pltpu.PrefetchScalarGridSpec(
-            num_scalar_prefetch=1,
-            grid=(2,),
-            in_specs=[whole] * 2 + [slab] * 2 + [result] * len(more),
-            out_specs=result,
-        ),
+        functools.partial(base_kernel, count, before is not None),
+        in_specs=[pl.BlockSpec(memory_space=pltpu.SMEM)] + in_hbm(count + 2 + len(more)),
+        out_specs=in_hbm(1)[0],
         out_shape=jax.ShapeDtypeStruct((total, 2 * columns), F32),
-        compiler_params=params(20),
-        cost_estimate=cost(8 * total * width * columns, 4 * total * width + 8 * width * columns),
+        scratch_shapes=share_scratch(shares, columns)
+        + [pltpu.VMEM((total, 2 * columns), F32), pltpu.SemaphoreType.DMA((3,))],
+        compiler_params=params(60),
+        cost_estimate=cost(0, 0),
         name="base",
     )(places, *shares, key_weight, value_weight, *more)
 
@@ -249,9 +316,19 @@
         jnp.dot(weights, v_ref[r, :, head], preferred_element_type=F32)
         for (r, mine, head), (weights, top, norm) in zip(pieces, shares)
     ]
+    @pl.when(first == 0)
+    def _():
+        lse_ref[...] = jnp.zeros_like(lse_ref)
+
+    logs = [[] for _ in range(rows)]
     for (r, mine, head), (weights, top, norm), value in zip(pieces, shares, mixed):
         out_ref[r, mine, :] = value / norm
-        lse_ref[r, mine, :] = jnp.broadcast_to(top + jnp.log(norm), (per_group, LANES))
+        logs[r].append(top + jnp.log(norm))
+    table = lse_ref[...]
+    at = lax.broadcasted_iota(jnp.int32, table.shape, 1)
+    for r in range(rows):
+        table = jnp.where(at == first + r, jnp.concatenate(logs[r], axis=0), table)
+    lse_ref[...] = table
 
 
 def stored(lengths, q_rows, keys, values):
@@ -260,109 +337,185 @@
     queries = q_rows.shape[1]
     block = pl.BlockSpec((rows, queries, HEAD_WIDTH), lambda i, n: (i, 0, 0))
     cache = pl.BlockSpec((rows, slots, width), lambda i, n: (i, 0, 0))
-    shape = jax.ShapeDtypeStruct((count, queries, HEAD_WIDTH), F32)
     return pl.pallas_call(
         functools.partial(stored_kernel, rows),
         grid_spec=pltpu.PrefetchScalarGridSpec(
             num_scalar_prefetch=1,
             grid=(count // rows,),
             in_specs=[block, cache, cache],
-            out_specs=(block, block),
+            out_specs=(block, pl.BlockSpec((queries, count), lambda i, n: (0, 0))),
         ),
-        out_shape=(shape, shape),
-        compiler_params=params(24),
+        out_shape=(
+            jax.ShapeDtypeStruct((count, queries, HEAD_WIDTH), F32),
+            jax.ShapeDtypeStruct((queries, count), F32),
+        ),
+        compiler_params=params(60),
         cost_estimate=cost(4 * count * queries * slots * HEAD_WIDTH, 4 * count * slots * width),
         name="stored",
     )(lengths, q_rows, keys, values)
 
 
-def final_kernel(
-    delivered_ref, sel_ref, base_ref, cos_ref, sin_ref, q_ref, old_ref, lse_ref, out_ref, key_ref, value_ref
-):
-    steps, block, wide = base_ref.shape
-    rows = steps * block
+def final_kernel(steps, count, place_ref, *refs):
+    shares, refs = refs[:count], refs[count:]
+    key_weight, value_weight, refs = refs[0], refs[1], refs[2:]
+    small, base_hbm, q_hbm, old_hbm, out_hbm, key_hbm, value_hbm = refs[:5], *refs[5:11]
+    refs = refs[11:]
+    share_refs, weight_refs, share_sem = refs[:count], refs[count : 2 * count], refs[2 * count]
+    refs = refs[2 * count + 1 :]
+    small_refs, small_sem, refs = refs[:5], refs[5], refs[6:]
+    base_ref, q_ref, old_ref, out_ref, key_ref, value_ref, in_sem, out_sem, new_sem = refs
+    delivered_ref, sel_ref, cos_ref, sin_ref, lse_ref = small_refs
+    total, wide = base_ref.shape
+    rows_dev = total // steps
     columns = wide // 2
     groups = columns // HEAD_WIDTH
     heads = q_ref.shape[2] // columns
+    block = min(rows_dev, LANES // steps)
+    here = steps * block
+    blocks = [slice(start, start + block) for start in range(0, rows_dev, block)]
     scale = 1.0 / math.sqrt(HEAD_WIDTH)
-    sel = sel_ref[...].reshape(rows, sel_ref.shape[2])
-    summed = base_ref[...].reshape(rows, wide) + jnp.dot(sel, delivered_ref[...], preferred_element_type=F32)
-    cos = cos_ref[...].reshape(rows, HEAD_WIDTH)
-    sin = sin_ref[...].reshape(rows, HEAD_WIDTH)
-    ones = jnp.ones((rows, LANES), BF16)
+    early = [pltpu.make_async_copy(a, b, small_sem.at[i]) for i, (a, b) in enumerate(zip(small, small_refs))]
+    fetch_base = pltpu.make_async_copy(base_hbm, base_ref, in_sem.at[2 * len(blocks)])
+    copies = share_copies(place_ref, shares, key_weight, value_weight, share_refs, weight_refs, share_sem)
+    for copy in early[:2] + [fetch_base] + sum(copies, []) + early[2:]:
+        copy.start()
+    fetches = []
+    for b, rows in enumerate(blocks):
+        fetches.append(
+            (
+                pltpu.make_async_copy(q_hbm.at[:, rows, :], q_ref.at[:, rows, :], in_sem.at[2 * b]),
+                pltpu.make_async_copy(old_hbm.at[:, rows, :], old_ref.at[:, rows, :], in_sem.at[2 * b + 1]),
+            )
+        )
+        for fetch in fetches[-1]:
+            fetch.start()
+
+    for copy in early[:2]:
+        copy.wait()
+    delta = jnp.dot(sel_ref[...], delivered_ref[...], preferred_element_type=F32)
+    fetch_base.wait()
+    summed = base_ref[...] + delta
+    halves = [summed[:, :columns], summed[:, columns:]]
+    for i in range(count):
+        copies[i][0].wait()
+        for number in range(2):
+            copies[i][1 + number].wait()
+            halves[number] += jnp.dot(share_refs[i][...], weight_refs[i][number], preferred_element_type=F32)
+    for copy in early[2:]:
+        copy.wait()
+    ones = jnp.ones((total, LANES), BF16)
     keys, both = [], []
     for g in range(groups):
         head = slice(g * HEAD_WIDTH, (g + 1) * HEAD_WIDTH)
-        piece = summed[:, head]
-        turned = (piece * cos + pltpu.roll(piece, HEAD_WIDTH // 2, 1) * sin).astype(BF16)
-        keys.append(turned)
-        key_ref[:, :, head] = turned.reshape(steps, block, HEAD_WIDTH)
-        fresh = summed[:, columns + g * HEAD_WIDTH : columns + (g + 1) * HEAD_WIDTH].astype(BF16)
+        piece = halves[0][:, head]
+        turned = piece * cos_ref[...] + pltpu.roll(piece, HEAD_WIDTH // 2, 1) * sin_ref[...]
+        keys.append(turned.astype(BF16))
+        key_ref[:, head] = keys[-1]
+        fresh = halves[1][:, head].astype(BF16)
+        value_ref[:, head] = fresh
         both.append(jnp.concatenate([fresh, ones], axis=1))
-        value_ref[:, :, head] = fresh.reshape(steps, block, HEAD_WIDTH)
-    sub = lax.broadcasted_iota(jnp.int32, (heads * block, rows), 0)
-    lane = lax.broadcasted_iota(jnp.int32, (heads * block, rows), 1)
+    sends = [
+        pltpu.make_async_copy(key_ref, key_hbm, new_sem.at[0]),
+        pltpu.make_async_copy(value_ref, value_hbm, new_sem.at[1]),
+    ]
+    for send in sends:
+        send.start()
+
+    sub = lax.broadcasted_iota(jnp.int32, (heads * block, here), 0)
+    lane = lax.broadcasted_iota(jnp.int32, (heads * block, here), 1)
     same_row = lax.rem(sub, block) == lax.rem(lane, block)
     of_step = lax.div(lane, block)
-    pieces = [(g, t) for g in range(groups) for t in range(steps)]
+    first_key = same_row & (of_step == 0)
+    all_ones = jnp.ones((here, LANES), BF16)
+    pieces = [(g, t) for t in range(steps) for g in range(groups)]
 
     def lanes(g, h):
         return slice((g * heads + h) * HEAD_WIDTH, (g * heads + h + 1) * HEAD_WIDTH)
 
-    raw = []
-    for g, t in pieces:
-        q = jnp.concatenate([q_ref[t, :, lanes(g, h)] for h in range(heads)], axis=0)
-        raw.append(lax.dot_general(q, keys[g], (((1,), (1,)), ((), ())), preferred_element_type=F32))
-    shares = []
-    for (g, t), scores in zip(pieces, raw):
-        first = (g * steps + t) * heads
-        lse = lse_ref[first : first + heads].reshape(heads * block, LANES)
-        scores = jnp.where(same_row & (of_step <= t), scores * scale, masked_score)
-        top = jnp.maximum(lse, jnp.max(scores, axis=1, keepdims=True))
-        shares.append((jnp.exp(scores - top[:, :1]).astype(BF16), jnp.exp(lse - top)))
-    mixed = [jnp.dot(w, both[g], preferred_element_type=F32) for (g, t), (w, kept) in zip(pieces, shares)]
-    for (g, t), (w, kept), value in zip(pieces, shares, mixed):
-        first = (g * steps + t) * heads
-        old = old_ref[first : first + heads].reshape(heads * block, HEAD_WIDTH)
-        result = (old * kept + value[:, :HEAD_WIDTH]) / (kept + value[:, HEAD_WIDTH:])
-        result = result.astype(BF16)
-        for h in range(heads):
-            out_ref[t, :, lanes(g, h)] = result[h * block : (h + 1) * block]
-
-
-def final(delivered, sel, base_rows, cos, sin, queries, old, lse):
+    def of_block(array, rows):
+        return jnp.concatenate(
+            [array[s * rows_dev + rows.start : s * rows_dev + rows.stop] for s in range(steps)], axis=0
+        )
+
+    for b, rows in enumerate(blocks):
+        own_keys = [of_block(k, rows) for k in keys]
+        own_both = [of_block(v, rows) for v in both]
+        logs = lse_ref[:, rows]
+        logs = jnp.concatenate([logs] * steps, axis=1)
+        fetches[b][0].wait()
+        raw = []
+        for g, t in pieces:
+            q = jnp.concatenate([q_ref[t, rows, lanes(g, h)] for h in range(heads)], axis=0)
+            raw.append(lax.dot_general(q, own_keys[g], (((1,), (1,)), ((), ())), preferred_element_type=F32))
+        shares = []
+        for (g, t), scores in zip(pieces, raw):
+            first = (g * steps + t) * heads
+            lse = jnp.concatenate(
+                [jnp.broadcast_to(logs[first + h : first + h + 1], (block, here)) for h in range(heads)], axis=0
+            )
+            lse = jnp.where(first_key, lse, masked_score)
+            scores = jnp.where(same_row & (of_step <= t), scores * scale, masked_score)
+            top = jnp.max(jnp.maximum(lse, scores), axis=1, keepdims=True)
+            shares.append((jnp.exp(scores - top).astype(BF16), jnp.exp(lse - top).astype(BF16)))
+        mixed = [
+            (
+                jnp.dot(w, own_both[g], preferred_element_type=F32),
+                jnp.dot(kept, all_ones, preferred_element_type=F32),
+            )
+            for (g, t), (w, kept) in zip(pieces, shares)
+        ]
+        fetches[b][1].wait()
+        for (g, t), (value, kept) in zip(pieces, mixed):
+            first = (g * steps + t) * heads
+            old = old_ref[first : first + heads, rows, :].reshape(heads * block, HEAD_WIDTH)
+            result = (old * kept + value[:, :HEAD_WIDTH]) / (kept + value[:, HEAD_WIDTH:])
+            result = result.astype(BF16)
+            for h in range(heads):
+                out_ref[t, rows, lanes(g, h)] = result[h * block : (h + 1) * block]
+            if g == groups - 1:
+                send = pltpu.make_async_copy(
+                    out_ref.at[t, rows, :], out_hbm.at[t, rows, :], out_sem.at[b * steps + t]
+                )
+                send.start()
+                sends.append(send)
+    for send in sends:
+        send.wait()
+
+
+def final(places, shares, key_weight, value_weight, delivered, sel, cos, sin, lse, base_rows, queries, old):
     steps, rows_dev, width = queries.shape
-    wide = base_rows.shape[1]
-    slots = sel.shape[1]
-    block = min(rows_dev, LANES // steps)
-
-    def rows_of(last):
-        return pl.BlockSpec((steps, block, last), lambda i: (0, i, 0))
-
-    def shaped(array):
-        return array.reshape(steps, rows_dev, array.shape[-1])
-
-    stored_part = pl.BlockSpec((old.shape[0], block, LANES), lambda i: (0, i, 0))
-    fresh = jax.ShapeDtypeStruct((steps, rows_dev, wide // 2), BF16)
+    total, wide = base_rows.shape
+    blocks = rows_dev // min(rows_dev, LANES // steps)
+    fresh = (total, wide // 2)
+    count = len(shares)
+    small = (delivered, sel, cos, sin, lse)
     return pl.pallas_call(
-        final_kernel,
-        grid=(rows_dev // block,),
-        in_specs=[
-            pl.BlockSpec(delivered.shape, lambda i: (0, 0)),
-            rows_of(slots),
-            rows_of(wide),
-            rows_of(HEAD_WIDTH),
-            rows_of(HEAD_WIDTH),
-            rows_of(width),
-            stored_part,
-            stored_part,
+        functools.partial(final_kernel, steps, count),
+        in_specs=[pl.BlockSpec(memory_space=pltpu.SMEM)] + in_hbm(count + 10),
+        out_specs=tuple(in_hbm(3)),
+        out_shape=(
+            jax.ShapeDtypeStruct(queries.shape, BF16),
+            jax.ShapeDtypeStruct(fresh, BF16),
+            jax.ShapeDtypeStruct(fresh, BF16),
+        ),
+        scratch_shapes=share_scratch(shares, wide // 2)
+        + [pltpu.VMEM(array.shape, array.dtype) for array in small]
+        + [
+            pltpu.SemaphoreType.DMA((len(small),)),
+            pltpu.VMEM(base_rows.shape, F32),
+            pltpu.VMEM(queries.shape, BF16),
+            pltpu.VMEM(old.shape, F32),
+            pltpu.VMEM(queries.shape, BF16),
+            pltpu.VMEM(fresh, BF16),
+            pltpu.VMEM(fresh, BF16),
+            pltpu.SemaphoreType.DMA((2 * blocks + 1,)),
+            pltpu.SemaphoreType.DMA((blocks * steps,)),
+            pltpu.SemaphoreType.DMA((2,)),
         ],
-        out_specs=(rows_of(width), rows_of(wide // 2), rows_of(wide // 2)),
-        out_shape=(jax.ShapeDtypeStruct(queries.shape, BF16), fresh, fresh),
-        compiler_params=params(24),
+        compiler_params=params(59),
         cost_estimate=cost(1e9, 8 * MIB),
         name="final",
-    )(delivered, shaped(sel), shaped(base_rows), shaped(cos), shaped(sin), queries, old, lse)
+    )(places, *shares, key_weight, value_weight, *small, base_rows, queries, old)
 
 
 def swap(x, bit):
@@ -394,6 +547,7 @@
     odd = jnp.reshape(t % 2, (1,)).astype(jnp.int32)
 
     x = normed_input_rows.reshape(total, width)
+    cuts = (0, 0, 8 * width // 16, width)
     outgoing, sel = dispatch(adapter_index_rows, x, rows_dev, resident, replicas)
     landed = lax.all_to_all(outgoing, "rep", split_axis=0, concat_axis=0, tiled=True)
 
@@ -401,8 +555,6 @@
     q_rows = queries.reshape(steps, rows_dev, groups, heads, HEAD_WIDTH)
     q_rows = q_rows.transpose(1, 2, 0, 3, 4).reshape(rows_dev, groups * steps * heads, HEAD_WIDTH)
     old, lse = stored(cache_fill_length, q_rows, cached_key_store, cached_value_store)
-    old = old.transpose(1, 0, 2)
-    lse = lse.transpose(1, 0, 2)
 
     positions = (
         cache_fill_length[None, :] + jnp.arange(steps, dtype=jnp.int32)[:, None]
@@ -422,26 +574,36 @@
     )
 
     near = swap(x_near, 1)
-    base_rows = base(jnp.stack([t, t ^ 1]).astype(jnp.int32), (x, near), key_weight, value_weight)
+    home = jnp.stack([t, t ^ 1, t ^ 2, t ^ 3]).astype(jnp.int32) * width
+    across = home[2:]
+    base_rows = base(home[:2], (x, near), key_weight, value_weight)
     landed, old, lse, cos, sin, base_rows, factor = lax.optimization_barrier(
         (landed, old, lse, cos, sin, base_rows, factor)
     )
 
+    part1, _ = lax.optimization_barrier((x_near[:, cuts[1] : cuts[2]], landed))
+    far1 = swap(part1, 2)
     keep, send = down(odd, landed, adapter_down_weight, factor)
     part = keep + swap(send, 1)
+    part, far1 = lax.optimization_barrier((part, far1))
     arrived = swap(part.astype(BF16), 2)
-    x_far, arrived = lax.optimization_barrier((x, arrived))
-    far = swap(x_far, 2)
+    part2, _ = lax.optimization_barrier((x_near[:, cuts[2] :], arrived))
+    far2 = swap(part2, 2)
+    base_rows = base(across + cuts[1], (far1, swap(far1, 1)), key_weight, value_weight, base_rows)
     own = (part + arrived.astype(F32)).astype(BF16)
     other = swap(own, 1)
     returned = up(odd, own, other, landed, adapter_up_weight)
+    returned, far2, base_rows, old = lax.optimization_barrier((returned, far2, base_rows, old))
     delivered = lax.all_to_all(returned, "rep", split_axis=0, concat_axis=0, tiled=True)
-    far, _ = lax.optimization_barrier((far, returned))
-    far_near = swap(far, 1)
-    base_rows = base(
-        jnp.stack([t ^ 2, t ^ 3]).astype(jnp.int32), (far, far_near), key_weight, value_weight, base_rows
+
+    base_rows = base(across + cuts[2], (far2, swap(far2, 1)), key_weight, value_weight, base_rows)
+    old = old.transpose(1, 0, 2)
+    base_rows, old, delivered = lax.optimization_barrier((base_rows, old, delivered))
+    out, keys, values = final(
+        across, (), key_weight, value_weight,
+        delivered, sel, cos, sin, lse, base_rows, queries, old,
     )
-    return final(delivered, sel, base_rows, cos, sin, queries, old, lse)
+    return out, keys.reshape(steps, rows_dev, columns), values.reshape(steps, rows_dev, columns)
 
 
 def solution(mesh):

time: 115 us -> 102 us (0.89)
  local copies, waits for them, and re-layouts: 32.2 us -> 9.86 us
  Pallas kernels: 22.6 us -> 42.7 us
  waiting for transfers between devices: 33.2 us -> 14.7 us
  starting transfers between devices: 24.5 us -> 31.3 us
  other arithmetic: 0.98 us -> 2.27 us
    unnamed x59 -> x27, local copies, waits for them, and re-layouts: 27.4 us -> 4.85 us
    ppermute x6 -> x8, waiting for transfers between devices: 25.3 us -> 4.11 us  [swap(): return lax.ppermute(x, 'tp', [(i, i ^ bit) for i in range(count)])]
    pallas_call x4 -> x5, Pallas kernels: 11.7 us -> 25.2 us  [the longest x3 16 us: base(): pl.pallas_call(functools.partial(base_kernel, count, before is not None),...]
    ppermute x6 -> x8, starting transfers between devices: 7.86 us -> 15 us  [swap(): return lax.ppermute(x, 'tp', [(i, i ^ bit) for i in range(count)])]
    pallas_call x1, Pallas kernels: 6.25 us -> 12.8 us  [stored(): pl.pallas_call(functools.partial(stored_kernel, rows), grid_spec=pltpu.Pr...]
    transpose x1 -> x0, local copies, waits for them, and re-layouts: 4.49 us -> none  [per_device(): lse = lse.transpose(1, 0, 2)]
    all_to_all x1, waiting for transfers between devices: 1.31 us -> 5.07 us  [per_device(): lax.all_to_all(returned, 'rep', split_axis=0, concat_axis=0, tiled=True)]
    optimization_barrier x0 -> x1, local copies, waits for them, and re-layouts: none -> 2.58 us  [per_device(): lax.optimization_barrier((returned, far2, base_rows, old))]
  transfers between devices with their start and end apart: 8 -> 10, of which waited for: 6 -> 6; matrix products, arithmetic and copies ran while one was open for 5% -> 7% of each run, Pallas kernels for 11% -> 33%
where the time goes in v1:
time: 102 us
  Pallas kernels  42.7 us (42%)
  starting transfers between devices  31.3 us (31%)
  waiting for transfers between devices  14.7 us (14%)
  local copies, waits for them, and re-layouts  9.86 us (10%)
  other arithmetic  2.27 us (2%)
    pallas_call x3, Pallas kernels, base(): pl.pallas_call(functools.partial(base_kernel, count, before is not None),...  16 us
    ppermute x8, starting transfers between devices, swap(): return lax.ppermute(x, 'tp', [(i, i ^ bit) for i in range(count)])  15 us
    pallas_call x1, Pallas kernels, stored(): pl.pallas_call(functools.partial(stored_kernel, rows), grid_spec=pltpu.Pr...  12.8 us
    all_to_all x1, starting transfers between devices, per_device(): lax.all_to_all(outgoing, 'rep', split_axis=0, concat_axis=0, tiled=True)  11.4 us
    pallas_call x1, Pallas kernels, final(): pl.pallas_call(functools.partial(final_kernel, steps, count), in_specs=[p...  5.86 us
    all_to_all x1, waiting for transfers between devices, per_device(): lax.all_to_all(outgoing, 'rep', split_axis=0, concat_axis=0, tiled=True)  5.54 us
    all_to_all x1, waiting for transfers between devices, per_device(): lax.all_to_all(returned, 'rep', split_axis=0, concat_axis=0, tiled=True)  5.07 us
    all_to_all x1, starting transfers between devices, per_device(): lax.all_to_all(returned, 'rep', split_axis=0, concat_axis=0, tiled=True)  4.92 us
  transfers between devices with their start and end apart: 10, of which 6 were waited for; matrix products, arithmetic and copies ran while one was open for 7% of the time, Pallas kernels for 33%

profile of v1, /device:TPU:1, one launch (start us, length us, event | category | flops | bytes accessed | tf_op | source)
XLA Modules:
  0.0 101.8 jit_solution(14872483853398778162)
XLA Ops:
  0.6 3.4 %dispatch.1 = (bf16[512,2176]{1,0:T(8,128)(2,1)}, bf16[256,512]{1,0:T(8,128)(2,1)}) custom-call(s32[4,64]{1,0:T(4,128)} %ids_hbm.1, bf16[256,2048]{1,0:T(8,128)(2,1)} %bitcast.28), custom_call_target="tpu_custom_call" | custom-call | flops 536870912 | bytes 3145728 | tf_op jit(solution)/shard_map/dispatch/pallas_call | solution.py:101
  4.1 11.4 %all-to-all-start = ((bf16[32,16,2176]{2,1,0:T(8,128)(2,1)}), bf16[32,16,2176]{2,1,0:T(8,128)(2,1)S(1)}, u32[]{:S(2)}, u32[]{:S(2)}) async-start(bf16[32,16,2176]{2,1,0:T(8,128)(2,1)} %bitcast.32), calls=%async_computation | async-start | bytes 4456448 | tf_op jit(solution)/shard_map/all_to_all | solution.py:552
  15.4 1.0 collective-permute-start
  16.7 1.3 %copy.14 = bf16[4,64,2,8,128]{4,3,0,2,1:T(8,128)(2,1)} copy(bf16[4,64,2,8,128]{4,3,2,1,0:T(8,128)(2,1)S(1)} %bitcast.27) | data formatting | bytes 2097152 | tf_op jit(solution)/shard_map/reshape | solution.py:555
  19.6 12.8 %stored.1 = (f32[64,64,128]{2,1,0:T(8,128)}, f32[64,64]{1,0:T(8,128)}) custom-call(s32[64]{0:T(128)} %length_ref.1, bf16[64,64,128]{2,1,0:T(8,128)(2,1)} %bitcast.26, bf16[64,256,256]{2,1,0:T(8,128)(2,1)} %k_ref.1, bf16[64,256,256]{2,1,0:T(8,128)(2,1)} %v_ref.1), custom_call_target="tpu_custom_call" | custom-call | flops 536870912 | bytes 16777216 | tf_op jit(solution)/shard_map/stored/pallas_call | solution.py:340
  33.1 1.1 %fusion.1 = (bf16[256,1024]{1,0:T(8,128)(2,1)}, bf16[256,1024]{1,0:T(8,128)(2,1)}) fusion(bf16[256,2048]{1,0:T(8,128)(2,1)S(1)} %bitcast.31), kind=kLoop, calls=%fused_computation.14 | loop fusion | bytes 2097152 | tf_op jit(solution)/shard_map/slice | solution.py:590
  34.1 6.6 %base.3.refs_4_ = f32[256,512]{1,0:T(8,128)} custom-call(s32[2]{0:T(128)} %get-tuple-element.66.place_ref, bf16[256,2048]{1,0:T(8,128)(2,1)} %bitcast.30, bf16[256,2048]{1,0:T(8,128)(2,1)} %collective-permute-done.refs_1_, bf16[8192,256]{1,0:T(8,128)(2,1)} %refs_0_.1, bf16[8192,256]{1,0:T(8,128)(2,1)} %refs_1_.1), custom_call_target="tpu_custom_call" | custom-call | tf_op jit(solution)/shard_map/base/pallas_call | solution.py:278
  40.7 5.5 %all-to-all-done = bf16[32,16,2176]{2,1,0:T(8,128)(2,1)S(1)} async-done(((bf16[32,16,2176]{2,1,0:T(8,128)(2,1)}), bf16[32,16,2176]{2,1,0:T(8,128)(2,1)S(1)}, u32[]{:S(2)}, u32[]{:S(2)}) %all-to-all-start) | async-done | bytes 2228256 | tf_op jit(solution)/shard_map/all_to_all | solution.py:552
  46.6 2.2 %copy-done.1 = bf16[4,2048,256]{2,1,0:T(8,128)(2,1)S(1)} copy-done((bf16[4,2048,256]{2,1,0:T(8,128)(2,1)S(1)}, bf16[4,2048,256]{2,1,0:T(8,128)(2,1)}, u32[]{:S(2)}) %copy-start.1) | copy-done | bytes 4194328
  48.8 3.1 %down.1 = (f32[256,256]{1,0:T(8,128)S(1)}, f32[256,256]{1,0:T(8,128)S(1)}) custom-call(s32[1]{0:T(128)} %bitcast.4.odd_ref, bf16[512,2176]{1,0:T(8,128)(2,1)S(1)} %bitcast.22, bf16[4,2048,256]{2,1,0:T(8,128)(2,1)S(1)} %copy-done.1, f32[4,1,256]{2,1,0:T(1,128)S(1)} %reshape.69.factor_ref), custom_call_target="tpu_custom_call" | custom-call | flops 2147483648 | bytes 6422528 | tf_op jit(solution)/shard_map/down/pallas_call | solution.py:153
  51.9 2.5 %collective-permute-start.1 = (f32[256,256]{1,0:T(8,128)S(1)}, f32[256,256]{1,0:T(8,128)S(1)}, u32[]{:S(2)}, u32[]{:S(2)}) collective-permute-start(f32[256,256]{1,0:T(8,128)S(1)} %get-tuple-element.40), channel_id=1, source_target_pairs={{0,1},{1,0},{2,3},{3,2},{4,5},{5,4},{6,7},{7,6},{8,9},{9,8},{10,11... | collective-permute-start | bytes 786440 | tf_op jit(solution)/shard_map/ppermute | solution.py:523
  54.5 1.2 %collective-permute-done.1 = f32[256,256]{1,0:T(8,128)S(1)} collective-permute-done((f32[256,256]{1,0:T(8,128)S(1)}, f32[256,256]{1,0:T(8,128)S(1)}, u32[]{:S(2)}, u32[]{:S(2)}) %collective-permute-start.1) | collective-permute-done | bytes 262176 | tf_op jit(solution)/shard_map/ppermute | solution.py:523
  55.7 1.8 %collective-permute-done.2.refs_0_ = bf16[256,1024]{1,0:T(8,128)(2,1)S(1)} collective-permute-done((bf16[256,1024]{1,0:T(8,128)(2,1)S(1)}, bf16[256,1024]{1,0:T(8,128)(2,1)S(1)}, u32[]{:S(2)}, u32[]{:S(2)}) %collective-permute-start.2) | collective-permute-done | bytes 524320 | tf_op jit(solution)/shard_map/ppermute | solution.py:523
  57.9 3.4 %collective-permute-start.6 = (bf16[256,1024]{1,0:T(8,128)(2,1)S(1)}, bf16[256,1024]{1,0:T(8,128)(2,1)S(1)}, u32[]{:S(2)}, u32[]{:S(2)}) collective-permute-start(bf16[256,1024]{1,0:T(8,128)(2,1)S(1)} %collective-permute-done.2.refs_0_), channel_id=1, source_target_pairs={{0,1},{1,0},{2,3},{3,2},{4,5},{5,4},{6,7},{7,6},{8,9},{9,8},{10,11... | collective-permute-start | bytes 1572872 | tf_op jit(solution)/shard_map/ppermute | solution.py:523
  61.4 1.0 collective-permute-start.5
  62.5 4.4 %collective-permute-start.4 = (bf16[256,256]{1,0:T(8,128)(2,1)S(1)}, bf16[256,256]{1,0:T(8,128)(2,1)S(1)}, u32[]{:S(2)}, u32[]{:S(2)}) collective-permute-start(bf16[256,256]{1,0:T(8,128)(2,1)S(1)} %add_convert_fusion.own_ref), channel_id=1, source_target_pairs={{0,1},{1,0},{2,3},{3,2},{4,5},{5,4},{6,7},{7,6},{8,9},{9,8},{10,11... | collective-permute-start | bytes 393224 | tf_op jit(solution)/shard_map/ppermute | solution.py:523
  67.9 1.6 %up.1 = bf16[512,512]{1,0:T(8,128)(2,1)} custom-call(s32[1]{0:T(128)} %bitcast.4.odd_ref, bf16[256,256]{1,0:T(8,128)(2,1)S(1)} %add_convert_fusion.own_ref, bf16[256,256]{1,0:T(8,128)(2,1)S(1)} %collective-permute-done.4.other_ref, bf16[512,2176]{1,0:T(8,128)(2,1)S(1)} %bitcast.23, bf16[4,2,128,256]{3,2,1,0:T(8,128)(2,1)S(1)} %copy-done), custom_call_target="tpu_custom_call" | custom-call | flops 268435456 | bytes 524288 | tf_op jit(solution)/shard_map/up/pallas_call | solution.py:194
  70.3 4.8 %base.4.refs_4_ = f32[256,512]{1,0:T(8,128)} custom-call(s32[2]{0:T(128)} %get-tuple-element.68.place_ref, bf16[256,1024]{1,0:T(8,128)(2,1)} %copy-done.8, bf16[256,1024]{1,0:T(8,128)(2,1)} %copy-done.9, bf16[8192,256]{1,0:T(8,128)(2,1)} %refs_0_.1, bf16[8192,256]{1,0:T(8,128)(2,1)} %refs_1_.1, f32[256,512]{1,0:T(8,128)} %base.3.refs_4_), custom_call_target="tpu_custom_call" | custom-call | tf_op jit(solution)/shard_map/base/pallas_call | solution.py:278
  75.1 1.9 %collective-permute-start.7 = (bf16[256,1024]{1,0:T(8,128)(2,1)}, bf16[256,1024]{1,0:T(8,128)(2,1)S(1)}, u32[]{:S(2)}, u32[]{:S(2)}) collective-permute-start(bf16[256,1024]{1,0:T(8,128)(2,1)} %collective-permute-done.5.refs_0_), channel_id=1, source_target_pairs={{0,1},{1,0},{2,3},{3,2},{4,5},{5,4},{6,7},{7,6},{8,9},{9,8},{10,11... | collective-permute-start | bytes 1572872 | tf_op jit(solution)/shard_map/ppermute | solution.py:523
  77.0 4.9 %all-to-all-start.1 = ((bf16[32,16,512]{2,1,0:T(8,128)(2,1)}), bf16[32,16,512]{2,1,0:T(8,128)(2,1)S(1)}, u32[]{:S(2)}, u32[]{:S(2)}) async-start(bf16[32,16,512]{2,1,0:T(8,128)(2,1)} %bitcast.11), calls=%async_computation.1 | async-start | bytes 1048576 | tf_op jit(solution)/shard_map/all_to_all | solution.py:597
  81.9 2.6 %copy.18 = f32[64,64,128]{2,0,1:T(8,128)} copy(f32[64,64,128]{2,1,0:T(8,128)S(1)} %copy-done.5) | data formatting | bytes 4194304 | tf_op jit(solution)/shard_map/optimization_barrier | solution.py:596
  85.3 4.6 %base.5.refs_7_ = f32[256,512]{1,0:T(8,128)} custom-call(s32[2]{0:T(128)} %get-tuple-element.67.place_ref, bf16[256,1024]{1,0:T(8,128)(2,1)} %collective-permute-done.5.refs_0_, bf16[256,1024]{1,0:T(8,128)(2,1)} %copy-done.10, bf16[8192,256]{1,0:T(8,128)(2,1)} %refs_0_.1, bf16[8192,256]{1,0:T(8,128)(2,1)} %refs_1_.1, f32[256,512]{1,0:T(8,128)} %base.4.refs_4_), custom_call_target="tpu_custom_call" | custom-call | tf_op jit(solution)/shard_map/base/pallas_call | solution.py:278
  89.9 5.1 %all-to-all-done.1 = bf16[32,16,512]{2,1,0:T(8,128)(2,1)S(1)} async-done(((bf16[32,16,512]{2,1,0:T(8,128)(2,1)}), bf16[32,16,512]{2,1,0:T(8,128)(2,1)S(1)}, u32[]{:S(2)}, u32[]{:S(2)}) %all-to-all-start.1) | async-done | bytes 524320 | tf_op jit(solution)/shard_map/all_to_all | solution.py:597
  95.8 5.9 %final.1 = (bf16[4,64,2048]{2,1,0:T(8,128)(2,1)}, bf16[256,256]{1,0:T(8,128)(2,1)}, bf16[256,256]{1,0:T(8,128)(2,1)}) custom-call(s32[2]{0:T(128)} %get-tuple-element.68.place_ref, bf16[8192,256]{1,0:T(8,128)(2,1)} %refs_0_.1, bf16[8192,256]{1,0:T(8,128)(2,1)} %refs_1_.1, bf16[512,512]{1,0:T(8,128)(2,1)} %bitcast.33, ...), custom_call_target="tpu_custom_call" | custom-call | flops 1000000000 | bytes 8388608 | tf_op jit(solution)/shard_map/final/pallas_call | solution.py:492
  (48 shorter events, 6.9 us)
Async XLA Ops:
  0.6 15.8 %copy-start.2 = (bf16[4,64,2048]{2,1,0:T(8,128)(2,1)S(1)}, bf16[4,64,2048]{2,1,0:T(8,128)(2,1)}, u32[]{:S(2)}) copy-start(bf16[4,64,2048]{2,1,0:T(8,128)(2,1)} %refs_8_) | copy-start | bytes 3145732
  4.1 13.9 %copy-start.11 = (s32[64]{0:T(128)S(1)}, s32[64]{0:T(128)}, u32[]{:S(2)}) copy-start(s32[64]{0:T(128)} %length_ref.1) | copy-start | bytes 772
  4.1 42.2 %all-to-all-start = ((bf16[32,16,2176]{2,1,0:T(8,128)(2,1)}), bf16[32,16,2176]{2,1,0:T(8,128)(2,1)S(1)}, u32[]{:S(2)}, u32[]{:S(2)}) async-start(bf16[32,16,2176]{2,1,0:T(8,128)(2,1)} %bitcast.32), calls=%async_computation | async-start | bytes 4456448 | tf_op jit(solution)/shard_map/all_to_all | solution.py:552
  15.4 18.7 %collective-permute-start = (bf16[256,2048]{1,0:T(8,128)(2,1)}, bf16[256,2048]{1,0:T(8,128)(2,1)}, u32[]{:S(2)}, u32[]{:S(2)}) collective-permute-start(bf16[256,2048]{1,0:T(8,128)(2,1)} %bitcast.29), channel_id=1, source_target_pairs={{0,1},{1,0},{2,3},{3,2},{4,5},{5,4},{6,7},{7,6},{8,9},{9,8},{10,11... | collective-permute-start | bytes 3145736 | tf_op jit(solution)/shard_map/ppermute | solution.py:523
  19.6 12.8 %copy-start.12 = (s32[4]{0:T(128)S(1)}, s32[4]{0:T(128)}, u32[]{:S(2)}) copy-start(s32[4]{0:T(128)} %param.20) | copy-start | bytes 52
  19.6 13.5 %copy-start.3 = (bf16[4,64,2048]{2,1,0:T(8,128)(2,1)S(1)}, bf16[4,64,2048]{2,1,0:T(8,128)(2,1)}, u32[]{:S(2)}) copy-start(bf16[4,64,2048]{2,1,0:T(8,128)(2,1)} %param.11) | copy-start | bytes 3145732
  34.1 12.1 %copy-start.7 = (bf16[256,1024]{1,0:T(8,128)(2,1)S(1)}, bf16[256,1024]{1,0:T(8,128)(2,1)}, u32[]{:S(2)}) copy-start(bf16[256,1024]{1,0:T(8,128)(2,1)} %get-tuple-element.41) | copy-start | bytes 1572868
  46.2 11.3 %collective-permute-start.2 = (bf16[256,1024]{1,0:T(8,128)(2,1)S(1)}, bf16[256,1024]{1,0:T(8,128)(2,1)S(1)}, u32[]{:S(2)}, u32[]{:S(2)}) collective-permute-start(bf16[256,1024]{1,0:T(8,128)(2,1)S(1)} %copy-done.7), channel_id=1, source_target_pairs={{0,2},{1,3},{2,0},{3,1},{4,6},{5,7},{6,4},{7,5},{8,10},{9,11},{10,... | collective-permute-start | bytes 1572872 | tf_op jit(solution)/shard_map/ppermute | solution.py:523
  46.6 2.2 %copy-start.1 = (bf16[4,2048,256]{2,1,0:T(8,128)(2,1)S(1)}, bf16[4,2048,256]{2,1,0:T(8,128)(2,1)}, u32[]{:S(2)}) copy-start(bf16[4,2048,256]{2,1,0:T(8,128)(2,1)} %weight_ref.2) | copy-start | bytes 12582916
  48.8 12.6 %copy-start.6 = (bf16[256,1024]{1,0:T(8,128)(2,1)S(1)}, bf16[256,1024]{1,0:T(8,128)(2,1)}, u32[]{:S(2)}) copy-start(bf16[256,1024]{1,0:T(8,128)(2,1)} %get-tuple-element.43) | copy-start | bytes 1572868
  48.8 19.1 %copy-start = (bf16[4,2,128,256]{3,2,1,0:T(8,128)(2,1)S(1)}, bf16[4,2,128,256]{3,2,1,0:T(8,128)(2,1)}, u32[]{:S(2)}) copy-start(bf16[4,2,128,256]{3,2,1,0:T(8,128)(2,1)} %weight_ref.3) | copy-start | bytes 1572868
  51.9 3.7 %collective-permute-start.1 = (f32[256,256]{1,0:T(8,128)S(1)}, f32[256,256]{1,0:T(8,128)S(1)}, u32[]{:S(2)}, u32[]{:S(2)}) collective-permute-start(f32[256,256]{1,0:T(8,128)S(1)} %get-tuple-element.40), channel_id=1, source_target_pairs={{0,1},{1,0},{2,3},{3,2},{4,5},{5,4},{6,7},{7,6},{8,9},{9,8},{10,11... | collective-permute-start | bytes 786440 | tf_op jit(solution)/shard_map/ppermute | solution.py:523
  57.5 12.8 %copy-start.8 = (bf16[256,1024]{1,0:T(8,128)(2,1)}, bf16[256,1024]{1,0:T(8,128)(2,1)S(1)}, u32[]{:S(2)}) copy-start(bf16[256,1024]{1,0:T(8,128)(2,1)S(1)} %collective-permute-done.2.refs_0_) | copy-start | bytes 1572868
  57.5 3.9 %collective-permute-start.3 = (bf16[256,256]{1,0:T(8,128)(2,1)S(1)}, bf16[256,256]{1,0:T(8,128)(2,1)S(1)}, u32[]{:S(2)}, u32[]{:S(2)}) collective-permute-start(bf16[256,256]{1,0:T(8,128)(2,1)S(1)} %convert_element_type.25), channel_id=1, source_target_pairs={{0,2},{1,3},{2,0},{3,1},{4,6},{5,7},{6,4},{7,5},{8,10},{9,11},{10,... | collective-permute-start | bytes 393224 | tf_op jit(solution)/shard_map/ppermute | solution.py:523
  57.9 11.5 %collective-permute-start.6 = (bf16[256,1024]{1,0:T(8,128)(2,1)S(1)}, bf16[256,1024]{1,0:T(8,128)(2,1)S(1)}, u32[]{:S(2)}, u32[]{:S(2)}) collective-permute-start(bf16[256,1024]{1,0:T(8,128)(2,1)S(1)} %collective-permute-done.2.refs_0_), channel_id=1, source_target_pairs={{0,1},{1,0},{2,3},{3,2},{4,5},{5,4},{6,7},{7,6},{8,9},{9,8},{10,11... | collective-permute-start | bytes 1572872 | tf_op jit(solution)/shard_map/ppermute | solution.py:523
  61.4 13.6 %collective-permute-start.5 = (bf16[256,1024]{1,0:T(8,128)(2,1)S(1)}, bf16[256,1024]{1,0:T(8,128)(2,1)}, u32[]{:S(2)}, u32[]{:S(2)}) collective-permute-start(bf16[256,1024]{1,0:T(8,128)(2,1)S(1)} %copy-done.6), channel_id=1, source_target_pairs={{0,2},{1,3},{2,0},{3,1},{4,6},{5,7},{6,4},{7,5},{8,10},{9,11},{10,... | collective-permute-start | bytes 1572872 | tf_op jit(solution)/shard_map/ppermute | solution.py:523
  62.5 5.4 %collective-permute-start.4 = (bf16[256,256]{1,0:T(8,128)(2,1)S(1)}, bf16[256,256]{1,0:T(8,128)(2,1)S(1)}, u32[]{:S(2)}, u32[]{:S(2)}) collective-permute-start(bf16[256,256]{1,0:T(8,128)(2,1)S(1)} %add_convert_fusion.own_ref), channel_id=1, source_target_pairs={{0,1},{1,0},{2,3},{3,2},{4,5},{5,4},{6,7},{7,6},{8,9},{9,8},{10,11... | collective-permute-start | bytes 393224 | tf_op jit(solution)/shard_map/ppermute | solution.py:523
  69.4 0.8 copy-start.9
  70.3 11.6 %copy-start.5 = (f32[64,64,128]{2,1,0:T(8,128)S(1)}, f32[64,64,128]{2,1,0:T(8,128)}, u32[]{:S(2)}) copy-start(f32[64,64,128]{2,1,0:T(8,128)} %get-tuple-element.49) | copy-start | bytes 6291460
  75.1 9.4 %collective-permute-start.7 = (bf16[256,1024]{1,0:T(8,128)(2,1)}, bf16[256,1024]{1,0:T(8,128)(2,1)S(1)}, u32[]{:S(2)}, u32[]{:S(2)}) collective-permute-start(bf16[256,1024]{1,0:T(8,128)(2,1)} %collective-permute-done.5.refs_0_), channel_id=1, source_target_pairs={{0,1},{1,0},{2,3},{3,2},{4,5},{5,4},{6,7},{7,6},{8,9},{9,8},{10,11... | collective-permute-start | bytes 1572872 | tf_op jit(solution)/shard_map/ppermute | solution.py:523
  77.0 18.0 %all-to-all-start.1 = ((bf16[32,16,512]{2,1,0:T(8,128)(2,1)}), bf16[32,16,512]{2,1,0:T(8,128)(2,1)S(1)}, u32[]{:S(2)}, u32[]{:S(2)}) async-start(bf16[32,16,512]{2,1,0:T(8,128)(2,1)} %bitcast.11), calls=%async_computation.1 | async-start | bytes 1048576 | tf_op jit(solution)/shard_map/all_to_all | solution.py:597
  84.5 0.8 copy-start.10
  95.0 0.8 copy-start.4

commit v2 on v1

--- a/solution.py
+++ b/solution.py
@@ -547,7 +547,7 @@
     odd = jnp.reshape(t % 2, (1,)).astype(jnp.int32)
 
     x = normed_input_rows.reshape(total, width)
-    cuts = (0, 0, 8 * width // 16, width)
+    cuts = (0, 7 * width // 16, 10 * width // 16, width)
     outgoing, sel = dispatch(adapter_index_rows, x, rows_dev, resident, replicas)
     landed = lax.all_to_all(outgoing, "rep", split_axis=0, concat_axis=0, tiled=True)
 
@@ -581,26 +581,32 @@
         (landed, old, lse, cos, sin, base_rows, factor)
     )
 
-    part1, _ = lax.optimization_barrier((x_near[:, cuts[1] : cuts[2]], landed))
-    far1 = swap(part1, 2)
+    part0, _ = lax.optimization_barrier((x_near[:, : cuts[1]], landed))
+    far0 = swap(part0, 2)
     keep, send = down(odd, landed, adapter_down_weight, factor)
     part = keep + swap(send, 1)
-    part, far1 = lax.optimization_barrier((part, far1))
+    part, far0 = lax.optimization_barrier((part, far0))
     arrived = swap(part.astype(BF16), 2)
-    part2, _ = lax.optimization_barrier((x_near[:, cuts[2] :], arrived))
-    far2 = swap(part2, 2)
-    base_rows = base(across + cuts[1], (far1, swap(far1, 1)), key_weight, value_weight, base_rows)
+    part1, _ = lax.optimization_barrier((x_near[:, cuts[1] : cuts[2]], arrived))
+    far1 = swap(part1, 2)
     own = (part + arrived.astype(F32)).astype(BF16)
     other = swap(own, 1)
     returned = up(odd, own, other, landed, adapter_up_weight)
-    returned, far2, base_rows, old = lax.optimization_barrier((returned, far2, base_rows, old))
+    returned, far0, far1, old, part2 = lax.optimization_barrier((returned, far0, far1, old, x_near[:, cuts[2] :]))
     delivered = lax.all_to_all(returned, "rep", split_axis=0, concat_axis=0, tiled=True)
 
-    base_rows = base(across + cuts[2], (far2, swap(far2, 1)), key_weight, value_weight, base_rows)
+    far2 = swap(part2, 2)
+    base_rows = base(
+        jnp.concatenate([across, across + cuts[1]]),
+        (far0, swap(far0, 1), far1, swap(far1, 1)),
+        key_weight, value_weight, base_rows,
+    )
     old = old.transpose(1, 0, 2)
-    base_rows, old, delivered = lax.optimization_barrier((base_rows, old, delivered))
+    base_rows, old, far2 = lax.optimization_barrier((base_rows, old, far2))
+    far2_near = swap(far2, 1)
+    base_rows, old, far2_near, delivered = lax.optimization_barrier((base_rows, old, far2_near, delivered))
     out, keys, values = final(
-        across, (), key_weight, value_weight,
+        across + cuts[2], (far2, far2_near), key_weight, value_weight,
         delivered, sel, cos, sin, lse, base_rows, queries, old,
     )
     return out, keys.reshape(steps, rows_dev, columns), values.reshape(steps, rows_dev, columns)

time: 102 us -> 99.4 us (0.975)
  local copies, waits for them, and re-layouts: 9.86 us -> 13 us
  waiting for transfers between devices: 14.7 us -> 11.6 us
  Pallas kernels: 42.7 us -> 39.7 us
    pallas_call x3 -> x2, Pallas kernels: 16 us -> 11.6 us  [base(): pl.pallas_call(functools.partial(base_kernel, count, before is not None),...]
    all_to_all x1, waiting for transfers between devices: 5.07 us -> 0.81 us  [per_device(): lax.all_to_all(returned, 'rep', split_axis=0, concat_axis=0, tiled=True)]
    ppermute x8 -> x10, waiting for transfers between devices: 4.11 us -> 6.08 us  [swap(): return lax.ppermute(x, 'tp', [(i, i ^ bit) for i in range(count)])]
    optimization_barrier x1, local copies, waits for them, and re-layouts: 2.58 us -> 4.14 us  [per_device(): lax.optimization_barrier((returned, far0, far1, old, x_near[:, cuts[2]:]))]
    pallas_call x1, Pallas kernels: 5.86 us -> 7.16 us  [final(): pl.pallas_call(functools.partial(final_kernel, steps, count), in_specs=[p...]
    unnamed x27 -> x25, local copies, waits for them, and re-layouts: 4.85 us -> 5.86 us
    ppermute x8 -> x10, starting transfers between devices: 15 us -> 14.2 us  [swap(): return lax.ppermute(x, 'tp', [(i, i ^ bit) for i in range(count)])]
  transfers between devices with their start and end apart: 10 -> 12, of which waited for: 6 -> 7; matrix products, arithmetic and copies ran while one was open for 7% -> 12% of each run, Pallas kernels for 33% -> 29%
where the time goes in v2:
time: 99.4 us; the launch traced here: 98.8 us
  Pallas kernels  39.7 us (40%)
  starting transfers between devices  30.7 us (31%)
  local copies, waits for them, and re-layouts  13 us (13%)
  waiting for transfers between devices  11.6 us (12%)
  other arithmetic  2.87 us (3%)
    ppermute x10, starting transfers between devices, swap(): return lax.ppermute(x, 'tp', [(i, i ^ bit) for i in range(count)])  14.2 us
    pallas_call x1, Pallas kernels, stored(): pl.pallas_call(functools.partial(stored_kernel, rows), grid_spec=pltpu.Pr...  12.8 us
    pallas_call x2, Pallas kernels, base(): pl.pallas_call(functools.partial(base_kernel, count, before is not None),...  11.6 us
    all_to_all x1, starting transfers between devices, per_device(): lax.all_to_all(outgoing, 'rep', split_axis=0, concat_axis=0, tiled=True)  11.4 us
    pallas_call x1, Pallas kernels, final(): pl.pallas_call(functools.partial(final_kernel, steps, count), in_specs=[p...  7.16 us
    ppermute x10, waiting for transfers between devices, swap(): return lax.ppermute(x, 'tp', [(i, i ^ bit) for i in range(count)])  6.08 us
    unnamed x25, local copies, waits for them, and re-layouts  5.86 us
    all_to_all x1, starting transfers between devices, per_device(): lax.all_to_all(returned, 'rep', split_axis=0, concat_axis=0, tiled=True)  5.17 us
  transfers between devices with their start and end apart: 12, of which 7 were waited for; matrix products, arithmetic and copies ran while one was open for 12% of the time, Pallas kernels for 29%

profile of v2, /device:TPU:1, one launch (start us, length us, event | category | flops | bytes accessed | tf_op | source)
XLA Modules:
  0.0 98.8 jit_solution(18024024842418289)
XLA Ops:
  0.6 3.4 %dispatch.1 = (bf16[512,2176]{1,0:T(8,128)(2,1)}, bf16[256,512]{1,0:T(8,128)(2,1)}) custom-call(s32[4,64]{1,0:T(4,128)} %ids_hbm.1, bf16[256,2048]{1,0:T(8,128)(2,1)} %bitcast.27), custom_call_target="tpu_custom_call" | custom-call | flops 536870912 | bytes 3145728 | tf_op jit(solution)/shard_map/dispatch/pallas_call | solution.py:101
  4.1 11.4 %all-to-all-start = ((bf16[32,16,2176]{2,1,0:T(8,128)(2,1)}), bf16[32,16,2176]{2,1,0:T(8,128)(2,1)S(1)}, u32[]{:S(2)}, u32[]{:S(2)}) async-start(bf16[32,16,2176]{2,1,0:T(8,128)(2,1)} %bitcast.34), calls=%async_computation | async-start | bytes 4456448 | tf_op jit(solution)/shard_map/all_to_all | solution.py:552
  15.4 1.0 %collective-permute-start = (bf16[256,2048]{1,0:T(8,128)(2,1)S(1)}, bf16[256,2048]{1,0:T(8,128)(2,1)}, u32[]{:S(2)}, u32[]{:S(2)}) collective-permute-start(bf16[256,2048]{1,0:T(8,128)(2,1)S(1)} %bitcast.29), channel_id=1, source_target_pairs={{0,1},{1,0},{2,3},{3,2},{4,5},{5,4},{6,7},{7,6},{8,9},{9,8},{10,11... | collective-permute-start | bytes 3145736 | tf_op jit(solution)/shard_map/ppermute | solution.py:523
  16.5 1.4 %copy.16 = bf16[32,8,16,128]{3,2,1,0:T(8,128)(2,1)S(1)} copy(bf16[32,8,16,128]{3,1,2,0:T(8,128)(2,1)} %bitcast.33) | data formatting | bytes 2097152
  17.9 1.3 %copy.14 = bf16[4,64,2,8,128]{4,3,0,2,1:T(8,128)(2,1)} copy(bf16[4,64,2,8,128]{4,3,2,1,0:T(8,128)(2,1)S(1)} %bitcast.26) | data formatting | bytes 2097152 | tf_op jit(solution)/shard_map/reshape | solution.py:555
  19.3 12.8 %stored.1 = (f32[64,64,128]{2,1,0:T(8,128)}, f32[64,64]{1,0:T(8,128)}) custom-call(s32[64]{0:T(128)} %length_ref.1, bf16[64,64,128]{2,1,0:T(8,128)(2,1)} %bitcast.25, bf16[64,256,256]{2,1,0:T(8,128)(2,1)} %k_ref.1, bf16[64,256,256]{2,1,0:T(8,128)(2,1)} %v_ref.1), custom_call_target="tpu_custom_call" | custom-call | flops 536870912 | bytes 16777216 | tf_op jit(solution)/shard_map/stored/pallas_call | solution.py:340
  32.1 0.8 slice.17
  33.5 0.8 pad_maximum_fusion
  35.1 6.4 %base.2.refs_6_ = f32[256,512]{1,0:T(8,128)} custom-call(s32[2]{0:T(128)} %get-tuple-element.74.place_ref, bf16[256,2048]{1,0:T(8,128)(2,1)} %bitcast.28, bf16[256,2048]{1,0:T(8,128)(2,1)} %collective-permute-done.refs_1_, bf16[8192,256]{1,0:T(8,128)(2,1)} %refs_2_.3, bf16[8192,256]{1,0:T(8,128)(2,1)} %refs_3_.3), custom_call_target="tpu_custom_call" | custom-call | tf_op jit(solution)/shard_map/base/pallas_call | solution.py:278
  41.5 4.7 %all-to-all-done = bf16[32,16,2176]{2,1,0:T(8,128)(2,1)S(1)} async-done(((bf16[32,16,2176]{2,1,0:T(8,128)(2,1)}), bf16[32,16,2176]{2,1,0:T(8,128)(2,1)S(1)}, u32[]{:S(2)}, u32[]{:S(2)}) %all-to-all-start) | async-done | bytes 2228256 | tf_op jit(solution)/shard_map/all_to_all | solution.py:552
  46.6 2.2 %copy-done.1 = bf16[4,2048,256]{2,1,0:T(8,128)(2,1)S(1)} copy-done((bf16[4,2048,256]{2,1,0:T(8,128)(2,1)S(1)}, bf16[4,2048,256]{2,1,0:T(8,128)(2,1)}, u32[]{:S(2)}) %copy-start.1) | copy-done | bytes 4194328
  48.8 3.1 %down.1 = (f32[256,256]{1,0:T(8,128)S(1)}, f32[256,256]{1,0:T(8,128)S(1)}) custom-call(s32[1]{0:T(128)} %bitcast.4.odd_ref, bf16[512,2176]{1,0:T(8,128)(2,1)S(1)} %bitcast.22, bf16[4,2048,256]{2,1,0:T(8,128)(2,1)S(1)} %copy-done.1, f32[4,1,256]{2,1,0:T(1,128)S(1)} %reshape.69.factor_ref), custom_call_target="tpu_custom_call" | custom-call | flops 2147483648 | bytes 6422528 | tf_op jit(solution)/shard_map/down/pallas_call | solution.py:153
  52.0 2.5 %collective-permute-start.1 = (f32[256,256]{1,0:T(8,128)S(1)}, f32[256,256]{1,0:T(8,128)S(1)}, u32[]{:S(2)}, u32[]{:S(2)}) collective-permute-start(f32[256,256]{1,0:T(8,128)S(1)} %get-tuple-element.45), channel_id=1, source_target_pairs={{0,1},{1,0},{2,3},{3,2},{4,5},{5,4},{6,7},{7,6},{8,9},{9,8},{10,11... | collective-permute-start | bytes 786440 | tf_op jit(solution)/shard_map/ppermute | solution.py:523
  54.5 1.2 %collective-permute-done.1 = f32[256,256]{1,0:T(8,128)S(1)} collective-permute-done((f32[256,256]{1,0:T(8,128)S(1)}, f32[256,256]{1,0:T(8,128)S(1)}, u32[]{:S(2)}, u32[]{:S(2)}) %collective-permute-start.1) | collective-permute-done | bytes 262176 | tf_op jit(solution)/shard_map/ppermute | solution.py:523
  56.9 3.4 %collective-permute-done.3 = bf16[256,256]{1,0:T(8,128)(2,1)S(1)} collective-permute-done((bf16[256,256]{1,0:T(8,128)(2,1)S(1)}, bf16[256,256]{1,0:T(8,128)(2,1)S(1)}, u32[]{:S(2)}, u32[]{:S(2)}) %collective-permute-start.3) | collective-permute-done | bytes 131104 | tf_op jit(solution)/shard_map/ppermute | solution.py:523
  60.7 5.7 %collective-permute-start.4 = (bf16[256,256]{1,0:T(8,128)(2,1)S(1)}, bf16[256,256]{1,0:T(8,128)(2,1)S(1)}, u32[]{:S(2)}, u32[]{:S(2)}) collective-permute-start(bf16[256,256]{1,0:T(8,128)(2,1)S(1)} %add_convert_fusion.own_ref), channel_id=1, source_target_pairs={{0,1},{1,0},{2,3},{3,2},{4,5},{5,4},{6,7},{7,6},{8,9},{9,8},{10,11... | collective-permute-start | bytes 393224 | tf_op jit(solution)/shard_map/ppermute | solution.py:523
  66.4 0.8 slice.19
  67.4 1.6 %up.1 = bf16[512,512]{1,0:T(8,128)(2,1)} custom-call(s32[1]{0:T(128)} %bitcast.4.odd_ref, bf16[256,256]{1,0:T(8,128)(2,1)S(1)} %add_convert_fusion.own_ref, bf16[256,256]{1,0:T(8,128)(2,1)S(1)} %collective-permute-done.4.other_ref, bf16[512,2176]{1,0:T(8,128)(2,1)S(1)} %bitcast.23, bf16[4,2,128,256]{3,2,1,0:T(8,128)(2,1)S(1)} %copy-done), custom_call_target="tpu_custom_call" | custom-call | flops 268435456 | bytes 524288 | tf_op jit(solution)/shard_map/up/pallas_call | solution.py:194
  69.0 2.3 %collective-permute-start.6 = (bf16[256,896]{1,0:T(8,128)(2,1)}, bf16[256,896]{1,0:T(8,128)(2,1)S(1)}, u32[]{:S(2)}, u32[]{:S(2)}) collective-permute-start(bf16[256,896]{1,0:T(8,128)(2,1)} %collective-permute-done.2.refs_0_), channel_id=1, source_target_pairs={{0,1},{1,0},{2,3},{3,2},{4,5},{5,4},{6,7},{7,6},{8,9},{9,8},{10,11... | collective-permute-start | bytes 1376264 | tf_op jit(solution)/shard_map/ppermute | solution.py:523
  72.0 5.2 %all-to-all-start.1 = ((bf16[32,16,512]{2,1,0:T(8,128)(2,1)}), bf16[32,16,512]{2,1,0:T(8,128)(2,1)S(1)}, u32[]{:S(2)}, u32[]{:S(2)}) async-start(bf16[32,16,512]{2,1,0:T(8,128)(2,1)} %bitcast.11), calls=%async_computation.1 | async-start | bytes 1048576 | tf_op jit(solution)/shard_map/all_to_all | solution.py:596
  77.8 4.1 %copy.18 = f32[64,64,128]{2,0,1:T(8,128)} copy(f32[64,64,128]{2,1,0:T(8,128)} %get-tuple-element.54) | data formatting | bytes 4194304 | tf_op jit(solution)/shard_map/optimization_barrier | solution.py:595
  83.4 5.2 %base.3.refs_9_ = f32[256,512]{1,0:T(8,128)} custom-call(s32[4]{0:T(128)} %pad_add_fusion.place_ref, bf16[256,896]{1,0:T(8,128)(2,1)} %collective-permute-done.2.refs_0_, bf16[256,896]{1,0:T(8,128)(2,1)} %copy-done.5, bf16[256,384]{1,0:T(8,128)(2,1)} %copy-done.8, bf16[256,384]{1,0:T(8,128)(2,1)} %copy-done.9, bf16[8192,256]{1,0:T(8,128)(2,1)} %refs_2_.3, ...), custom_call_target="tpu_custom_call" | custom-call | tf_op jit(solution)/shard_map/base/pallas_call | solution.py:278
  89.4 0.8 all-to-all-done.1
  91.5 7.2 %final.1 = (bf16[4,64,2048]{2,1,0:T(8,128)(2,1)}, bf16[256,256]{1,0:T(8,128)(2,1)}, bf16[256,256]{1,0:T(8,128)(2,1)}) custom-call(s32[2]{0:T(128)} %get-tuple-element.75.place_ref, bf16[256,768]{1,0:T(8,128)(2,1)} %copy-done.6, bf16[256,768]{1,0:T(8,128)(2,1)} %copy-done.7, bf16[8192,256]{1,0:T(8,128)(2,1)} %refs_2_.3, bf16[8192,256]{1,0:T(8,128)(2,1)} %refs_3_.3, ...), custom_call_target="tpu_custom_call" | custom-call | flops 1000000000 | bytes 8388608 | tf_op jit(solution)/shard_map/final/pallas_call | solution.py:492
  (52 shorter events, 8.4 us)
Async XLA Ops:
  0.6 14.8 %copy-start.2 = (bf16[4,64,2048]{2,1,0:T(8,128)(2,1)S(1)}, bf16[4,64,2048]{2,1,0:T(8,128)(2,1)}, u32[]{:S(2)}) copy-start(bf16[4,64,2048]{2,1,0:T(8,128)(2,1)} %param.11) | copy-start | bytes 3145732
  4.1 15.2 %copy-start.10 = (s32[64]{0:T(128)S(1)}, s32[64]{0:T(128)}, u32[]{:S(2)}) copy-start(s32[64]{0:T(128)} %length_ref.1) | copy-start | bytes 772
  4.1 42.2 %all-to-all-start = ((bf16[32,16,2176]{2,1,0:T(8,128)(2,1)}), bf16[32,16,2176]{2,1,0:T(8,128)(2,1)S(1)}, u32[]{:S(2)}, u32[]{:S(2)}) async-start(bf16[32,16,2176]{2,1,0:T(8,128)(2,1)} %bitcast.34), calls=%async_computation | async-start | bytes 4456448 | tf_op jit(solution)/shard_map/all_to_all | solution.py:552
  15.4 19.6 %collective-permute-start = (bf16[256,2048]{1,0:T(8,128)(2,1)S(1)}, bf16[256,2048]{1,0:T(8,128)(2,1)}, u32[]{:S(2)}, u32[]{:S(2)}) collective-permute-start(bf16[256,2048]{1,0:T(8,128)(2,1)S(1)} %bitcast.29), channel_id=1, source_target_pairs={{0,1},{1,0},{2,3},{3,2},{4,5},{5,4},{6,7},{7,6},{8,9},{9,8},{10,11... | collective-permute-start | bytes 3145736 | tf_op jit(solution)/shard_map/ppermute | solution.py:523
  19.3 15.1 %copy-start.11 = (s32[4]{0:T(128)S(1)}, s32[4]{0:T(128)}, u32[]{:S(2)}) copy-start(s32[4]{0:T(128)} %param.20) | copy-start | bytes 52
  46.2 10.2 %collective-permute-start.2 = (bf16[256,896]{1,0:T(8,128)(2,1)}, bf16[256,896]{1,0:T(8,128)(2,1)}, u32[]{:S(2)}, u32[]{:S(2)}) collective-permute-start(bf16[256,896]{1,0:T(8,128)(2,1)} %slice.17), channel_id=1, source_target_pairs={{0,2},{1,3},{2,0},{3,1},{4,6},{5,7},{6,4},{7,5},{8,10},{9,11},{10,... | collective-permute-start | bytes 1376264 | tf_op jit(solution)/shard_map/ppermute | solution.py:523
  46.6 2.2 %copy-start.1 = (bf16[4,2048,256]{2,1,0:T(8,128)(2,1)S(1)}, bf16[4,2048,256]{2,1,0:T(8,128)(2,1)}, u32[]{:S(2)}) copy-start(bf16[4,2048,256]{2,1,0:T(8,128)(2,1)} %weight_ref.2) | copy-start | bytes 12582916
  48.8 8.1 %copy-start.3 = (bf16[4,64,2048]{2,1,0:T(8,128)(2,1)S(1)}, bf16[4,64,2048]{2,1,0:T(8,128)(2,1)}, u32[]{:S(2)}) copy-start(bf16[4,64,2048]{2,1,0:T(8,128)(2,1)} %param.11) | copy-start | bytes 3145732
  48.8 18.6 %copy-start = (bf16[4,2,128,256]{3,2,1,0:T(8,128)(2,1)S(1)}, bf16[4,2,128,256]{3,2,1,0:T(8,128)(2,1)}, u32[]{:S(2)}) copy-start(bf16[4,2,128,256]{3,2,1,0:T(8,128)(2,1)} %weight_ref.3) | copy-start | bytes 1572868
  52.0 3.7 %collective-permute-start.1 = (f32[256,256]{1,0:T(8,128)S(1)}, f32[256,256]{1,0:T(8,128)S(1)}, u32[]{:S(2)}, u32[]{:S(2)}) collective-permute-start(f32[256,256]{1,0:T(8,128)S(1)} %get-tuple-element.45), channel_id=1, source_target_pairs={{0,1},{1,0},{2,3},{3,2},{4,5},{5,4},{6,7},{7,6},{8,9},{9,8},{10,11... | collective-permute-start | bytes 786440 | tf_op jit(solution)/shard_map/ppermute | solution.py:523
  56.4 3.9 %collective-permute-start.3 = (bf16[256,256]{1,0:T(8,128)(2,1)S(1)}, bf16[256,256]{1,0:T(8,128)(2,1)S(1)}, u32[]{:S(2)}, u32[]{:S(2)}) collective-permute-start(bf16[256,256]{1,0:T(8,128)(2,1)S(1)} %convert_element_type.25), channel_id=1, source_target_pairs={{0,2},{1,3},{2,0},{3,1},{4,6},{5,7},{6,4},{7,5},{8,10},{9,11},{10,... | collective-permute-start | bytes 393224 | tf_op jit(solution)/shard_map/ppermute | solution.py:523
  60.3 8.7 %collective-permute-start.5 = (bf16[256,384]{1,0:T(8,128)(2,1)S(1)}, bf16[256,384]{1,0:T(8,128)(2,1)S(1)}, u32[]{:S(2)}, u32[]{:S(2)}) collective-permute-start(bf16[256,384]{1,0:T(8,128)(2,1)S(1)} %slice.18), channel_id=1, source_target_pairs={{0,2},{1,3},{2,0},{3,1},{4,6},{5,7},{6,4},{7,5},{8,10},{9,11},{10,... | collective-permute-start | bytes 589832 | tf_op jit(solution)/shard_map/ppermute | solution.py:523
  60.7 6.7 %collective-permute-start.4 = (bf16[256,256]{1,0:T(8,128)(2,1)S(1)}, bf16[256,256]{1,0:T(8,128)(2,1)S(1)}, u32[]{:S(2)}, u32[]{:S(2)}) collective-permute-start(bf16[256,256]{1,0:T(8,128)(2,1)S(1)} %add_convert_fusion.own_ref), channel_id=1, source_target_pairs={{0,1},{1,0},{2,3},{3,2},{4,5},{5,4},{6,7},{7,6},{8,9},{9,8},{10,11... | collective-permute-start | bytes 393224 | tf_op jit(solution)/shard_map/ppermute | solution.py:523
  69.0 12.9 %copy-start.8 = (bf16[256,384]{1,0:T(8,128)(2,1)}, bf16[256,384]{1,0:T(8,128)(2,1)S(1)}, u32[]{:S(2)}) copy-start(bf16[256,384]{1,0:T(8,128)(2,1)S(1)} %collective-permute-done.5.refs_2_) | copy-start | bytes 589828
  69.0 12.9 %collective-permute-start.6 = (bf16[256,896]{1,0:T(8,128)(2,1)}, bf16[256,896]{1,0:T(8,128)(2,1)S(1)}, u32[]{:S(2)}, u32[]{:S(2)}) collective-permute-start(bf16[256,896]{1,0:T(8,128)(2,1)} %collective-permute-done.2.refs_0_), channel_id=1, source_target_pairs={{0,1},{1,0},{2,3},{3,2},{4,5},{5,4},{6,7},{7,6},{8,9},{9,8},{10,11... | collective-permute-start | bytes 1376264 | tf_op jit(solution)/shard_map/ppermute | solution.py:523
  71.3 17.3 %collective-permute-start.8 = (bf16[256,768]{1,0:T(8,128)(2,1)}, bf16[256,768]{1,0:T(8,128)(2,1)S(1)}, u32[]{:S(2)}, u32[]{:S(2)}) collective-permute-start(bf16[256,768]{1,0:T(8,128)(2,1)} %slice.19), channel_id=1, source_target_pairs={{0,2},{1,3},{2,0},{3,1},{4,6},{5,7},{6,4},{7,5},{8,10},{9,11},{10,... | collective-permute-start | bytes 1179656 | tf_op jit(solution)/shard_map/ppermute | solution.py:523
  71.7 10.2 %collective-permute-start.7 = (bf16[256,384]{1,0:T(8,128)(2,1)S(1)}, bf16[256,384]{1,0:T(8,128)(2,1)S(1)}, u32[]{:S(2)}, u32[]{:S(2)}) collective-permute-start(bf16[256,384]{1,0:T(8,128)(2,1)S(1)} %collective-permute-done.5.refs_2_), channel_id=1, source_target_pairs={{0,1},{1,0},{2,3},{3,2},{4,5},{5,4},{6,7},{7,6},{8,9},{9,8},{10,11... | collective-permute-start | bytes 589832 | tf_op jit(solution)/shard_map/ppermute | solution.py:523
  72.0 18.2 %all-to-all-start.1 = ((bf16[32,16,512]{2,1,0:T(8,128)(2,1)}), bf16[32,16,512]{2,1,0:T(8,128)(2,1)S(1)}, u32[]{:S(2)}, u32[]{:S(2)}) async-start(bf16[32,16,512]{2,1,0:T(8,128)(2,1)} %bitcast.11), calls=%async_computation.1 | async-start | bytes 1048576 | tf_op jit(solution)/shard_map/all_to_all | solution.py:596
  81.9 0.7 copy-start.9
  82.6 0.8 copy-start.5
  88.6 2.1 %copy-start.6 = (bf16[256,768]{1,0:T(8,128)(2,1)}, bf16[256,768]{1,0:T(8,128)(2,1)S(1)}, u32[]{:S(2)}) copy-start(bf16[256,768]{1,0:T(8,128)(2,1)S(1)} %collective-permute-done.8.refs_0_) | copy-start | bytes 1179652
  88.6 2.1 %collective-permute-start.9 = (bf16[256,768]{1,0:T(8,128)(2,1)S(1)}, bf16[256,768]{1,0:T(8,128)(2,1)S(1)}, u32[]{:S(2)}, u32[]{:S(2)}) collective-permute-start(bf16[256,768]{1,0:T(8,128)(2,1)S(1)} %collective-permute-done.8.refs_0_), channel_id=1, source_target_pairs={{0,1},{1,0},{2,3},{3,2},{4,5},{5,4},{6,7},{7,6},{8,9},{9,8},{10,11... | collective-permute-start | bytes 1179656 | tf_op jit(solution)/shard_map/ppermute | solution.py:523
  90.2 0.8 copy-start.4
  90.7 0.7 copy-start.7

commit v3 on v2

--- a/solution.py
+++ b/solution.py
@@ -547,7 +547,7 @@
     odd = jnp.reshape(t % 2, (1,)).astype(jnp.int32)
 
     x = normed_input_rows.reshape(total, width)
-    cuts = (0, 7 * width // 16, 10 * width // 16, width)
+    cuts = (0, 5 * width // 16, 9 * width // 16, width)
     outgoing, sel = dispatch(adapter_index_rows, x, rows_dev, resident, replicas)
     landed = lax.all_to_all(outgoing, "rep", split_axis=0, concat_axis=0, tiled=True)
 

time: 99.4 us -> 97 us (0.976)
  starting transfers between devices: 30.7 us -> 29.3 us
    all_to_all x1, starting transfers between devices: 5.17 us -> 3.98 us  [per_device(): lax.all_to_all(returned, 'rep', split_axis=0, concat_axis=0, tiled=True)]
  transfers between devices with their start and end apart: 12 -> 12, of which waited for: 7 -> 7; matrix products, arithmetic and copies ran while one was open for 12% -> 12% of each run, Pallas kernels for 29% -> 30%
where the time goes in v3:
time: 97 us; the launch traced here: 96.4 us
  Pallas kernels  39.5 us (41%)
  starting transfers between devices  29.3 us (30%)
  local copies, waits for them, and re-layouts  13 us (13%)
  waiting for transfers between devices  10.8 us (11%)
  other arithmetic  2.86 us (3%)
  between operations  0.97 us (1%)
    ppermute x10, starting transfers between devices, swap(): return lax.ppermute(x, 'tp', [(i, i ^ bit) for i in range(count)])  13.9 us
    pallas_call x1, Pallas kernels, stored(): pl.pallas_call(functools.partial(stored_kernel, rows), grid_spec=pltpu.Pr...  12.8 us
    all_to_all x1, starting transfers between devices, per_device(): lax.all_to_all(outgoing, 'rep', split_axis=0, concat_axis=0, tiled=True)  11.4 us
    pallas_call x2, Pallas kernels, base(): pl.pallas_call(functools.partial(base_kernel, count, before is not None),...  11.2 us
    pallas_call x1, Pallas kernels, final(): pl.pallas_call(functools.partial(final_kernel, steps, count), in_specs=[p...  7.4 us
    unnamed x25, local copies, waits for them, and re-layouts  5.84 us
    ppermute x10, waiting for transfers between devices, swap(): return lax.ppermute(x, 'tp', [(i, i ^ bit) for i in range(count)])  5.39 us
    all_to_all x1, waiting for transfers between devices, per_device(): lax.all_to_all(outgoing, 'rep', split_axis=0, concat_axis=0, tiled=True)  4.74 us
  transfers between devices with their start and end apart: 12, of which 7 were waited for; matrix products, arithmetic and copies ran while one was open for 12% of the time, Pallas kernels for 30%

profile of v3, /device:TPU:1, one launch (start us, length us, event | category | flops | bytes accessed | tf_op | source)
XLA Modules:
  0.0 96.4 jit_solution(17569258860878640300)
XLA Ops:
  0.6 3.4 %dispatch.1 = (bf16[512,2176]{1,0:T(8,128)(2,1)}, bf16[256,512]{1,0:T(8,128)(2,1)}) custom-call(s32[4,64]{1,0:T(4,128)} %ids_hbm.1, bf16[256,2048]{1,0:T(8,128)(2,1)} %bitcast.27), custom_call_target="tpu_custom_call" | custom-call | flops 536870912 | bytes 3145728 | tf_op jit(solution)/shard_map/dispatch/pallas_call | solution.py:101
  4.1 11.4 %all-to-all-start = ((bf16[32,16,2176]{2,1,0:T(8,128)(2,1)}), bf16[32,16,2176]{2,1,0:T(8,128)(2,1)S(1)}, u32[]{:S(2)}, u32[]{:S(2)}) async-start(bf16[32,16,2176]{2,1,0:T(8,128)(2,1)} %bitcast.34), calls=%async_computation | async-start | bytes 4456448 | tf_op jit(solution)/shard_map/all_to_all | solution.py:552
  15.4 1.0 %collective-permute-start = (bf16[256,2048]{1,0:T(8,128)(2,1)S(1)}, bf16[256,2048]{1,0:T(8,128)(2,1)}, u32[]{:S(2)}, u32[]{:S(2)}) collective-permute-start(bf16[256,2048]{1,0:T(8,128)(2,1)S(1)} %bitcast.29), channel_id=1, source_target_pairs={{0,1},{1,0},{2,3},{3,2},{4,5},{5,4},{6,7},{7,6},{8,9},{9,8},{10,11... | collective-permute-start | bytes 3145736 | tf_op jit(solution)/shard_map/ppermute | solution.py:523
  16.5 1.4 %copy.16 = bf16[32,8,16,128]{3,2,1,0:T(8,128)(2,1)S(1)} copy(bf16[32,8,16,128]{3,1,2,0:T(8,128)(2,1)} %bitcast.33) | data formatting | bytes 2097152
  17.9 1.3 %copy.14 = bf16[4,64,2,8,128]{4,3,0,2,1:T(8,128)(2,1)} copy(bf16[4,64,2,8,128]{4,3,2,1,0:T(8,128)(2,1)S(1)} %bitcast.26) | data formatting | bytes 2097152 | tf_op jit(solution)/shard_map/reshape | solution.py:555
  19.3 12.8 %stored.1 = (f32[64,64,128]{2,1,0:T(8,128)}, f32[64,64]{1,0:T(8,128)}) custom-call(s32[64]{0:T(128)} %length_ref.1, bf16[64,64,128]{2,1,0:T(8,128)(2,1)} %bitcast.25, bf16[64,256,256]{2,1,0:T(8,128)(2,1)} %k_ref.1, bf16[64,256,256]{2,1,0:T(8,128)(2,1)} %v_ref.1), custom_call_target="tpu_custom_call" | custom-call | flops 536870912 | bytes 16777216 | tf_op jit(solution)/shard_map/stored/pallas_call | solution.py:340
  35.1 6.4 %base.2.refs_6_ = f32[256,512]{1,0:T(8,128)} custom-call(s32[2]{0:T(128)} %get-tuple-element.74.place_ref, bf16[256,2048]{1,0:T(8,128)(2,1)} %bitcast.28, bf16[256,2048]{1,0:T(8,128)(2,1)} %collective-permute-done.refs_1_, bf16[8192,256]{1,0:T(8,128)(2,1)} %refs_2_.3, bf16[8192,256]{1,0:T(8,128)(2,1)} %refs_3_.3), custom_call_target="tpu_custom_call" | custom-call | tf_op jit(solution)/shard_map/base/pallas_call | solution.py:278
  41.5 4.7 %all-to-all-done = bf16[32,16,2176]{2,1,0:T(8,128)(2,1)S(1)} async-done(((bf16[32,16,2176]{2,1,0:T(8,128)(2,1)}), bf16[32,16,2176]{2,1,0:T(8,128)(2,1)S(1)}, u32[]{:S(2)}, u32[]{:S(2)}) %all-to-all-start) | async-done | bytes 2228256 | tf_op jit(solution)/shard_map/all_to_all | solution.py:552
  46.6 2.2 %copy-done.1 = bf16[4,2048,256]{2,1,0:T(8,128)(2,1)S(1)} copy-done((bf16[4,2048,256]{2,1,0:T(8,128)(2,1)S(1)}, bf16[4,2048,256]{2,1,0:T(8,128)(2,1)}, u32[]{:S(2)}) %copy-start.1) | copy-done | bytes 4194328
  48.8 3.1 %down.1 = (f32[256,256]{1,0:T(8,128)S(1)}, f32[256,256]{1,0:T(8,128)S(1)}) custom-call(s32[1]{0:T(128)} %bitcast.4.odd_ref, bf16[512,2176]{1,0:T(8,128)(2,1)S(1)} %bitcast.22, bf16[4,2048,256]{2,1,0:T(8,128)(2,1)S(1)} %copy-done.1, f32[4,1,256]{2,1,0:T(1,128)S(1)} %reshape.69.factor_ref), custom_call_target="tpu_custom_call" | custom-call | flops 2147483648 | bytes 6422528 | tf_op jit(solution)/shard_map/down/pallas_call | solution.py:153
  52.0 2.5 %collective-permute-start.1 = (f32[256,256]{1,0:T(8,128)S(1)}, f32[256,256]{1,0:T(8,128)S(1)}, u32[]{:S(2)}, u32[]{:S(2)}) collective-permute-start(f32[256,256]{1,0:T(8,128)S(1)} %get-tuple-element.45), channel_id=1, source_target_pairs={{0,1},{1,0},{2,3},{3,2},{4,5},{5,4},{6,7},{7,6},{8,9},{9,8},{10,11... | collective-permute-start | bytes 786440 | tf_op jit(solution)/shard_map/ppermute | solution.py:523
  54.5 1.2 %collective-permute-done.1 = f32[256,256]{1,0:T(8,128)S(1)} collective-permute-done((f32[256,256]{1,0:T(8,128)S(1)}, f32[256,256]{1,0:T(8,128)S(1)}, u32[]{:S(2)}, u32[]{:S(2)}) %collective-permute-start.1) | collective-permute-done | bytes 262176 | tf_op jit(solution)/shard_map/ppermute | solution.py:523
  55.7 1.1 %collective-permute-start.3 = (bf16[256,256]{1,0:T(8,128)(2,1)S(1)}, bf16[256,256]{1,0:T(8,128)(2,1)S(1)}, u32[]{:S(2)}, u32[]{:S(2)}) collective-permute-start(bf16[256,256]{1,0:T(8,128)(2,1)S(1)} %convert_element_type.25), channel_id=1, source_target_pairs={{0,2},{1,3},{2,0},{3,1},{4,6},{5,7},{6,4},{7,5},{8,10},{9,11},{10,... | collective-permute-start | bytes 393224 | tf_op jit(solution)/shard_map/ppermute | solution.py:523
  56.9 2.7 %collective-permute-done.3 = bf16[256,256]{1,0:T(8,128)(2,1)S(1)} collective-permute-done((bf16[256,256]{1,0:T(8,128)(2,1)S(1)}, bf16[256,256]{1,0:T(8,128)(2,1)S(1)}, u32[]{:S(2)}, u32[]{:S(2)}) %collective-permute-start.3) | collective-permute-done | bytes 131104 | tf_op jit(solution)/shard_map/ppermute | solution.py:523
  59.6 2.0 %collective-permute-start.5 = (bf16[256,512]{1,0:T(8,128)(2,1)S(1)}, bf16[256,512]{1,0:T(8,128)(2,1)S(1)}, u32[]{:S(2)}, u32[]{:S(2)}) collective-permute-start(bf16[256,512]{1,0:T(8,128)(2,1)S(1)} %slice.18), channel_id=1, source_target_pairs={{0,2},{1,3},{2,0},{3,1},{4,6},{5,7},{6,4},{7,5},{8,10},{9,11},{10,... | collective-permute-start | bytes 786440 | tf_op jit(solution)/shard_map/ppermute | solution.py:523
  61.6 1.6 %collective-permute-start.4 = (bf16[256,256]{1,0:T(8,128)(2,1)S(1)}, bf16[256,256]{1,0:T(8,128)(2,1)S(1)}, u32[]{:S(2)}, u32[]{:S(2)}) collective-permute-start(bf16[256,256]{1,0:T(8,128)(2,1)S(1)} %add_convert_fusion.own_ref), channel_id=1, source_target_pairs={{0,1},{1,0},{2,3},{3,2},{4,5},{5,4},{6,7},{7,6},{8,9},{9,8},{10,11... | collective-permute-start | bytes 393224 | tf_op jit(solution)/shard_map/ppermute | solution.py:523
  64.2 1.6 %up.1 = bf16[512,512]{1,0:T(8,128)(2,1)} custom-call(s32[1]{0:T(128)} %bitcast.4.odd_ref, bf16[256,256]{1,0:T(8,128)(2,1)S(1)} %add_convert_fusion.own_ref, bf16[256,256]{1,0:T(8,128)(2,1)S(1)} %collective-permute-done.4.other_ref, bf16[512,2176]{1,0:T(8,128)(2,1)S(1)} %bitcast.23, bf16[4,2,128,256]{3,2,1,0:T(8,128)(2,1)S(1)} %copy-done), custom_call_target="tpu_custom_call" | custom-call | flops 268435456 | bytes 524288 | tf_op jit(solution)/shard_map/up/pallas_call | solution.py:194
  66.3 1.9 %collective-permute-start.8 = (bf16[256,896]{1,0:T(8,128)(2,1)}, bf16[256,896]{1,0:T(8,128)(2,1)S(1)}, u32[]{:S(2)}, u32[]{:S(2)}) collective-permute-start(bf16[256,896]{1,0:T(8,128)(2,1)} %slice.19), channel_id=1, source_target_pairs={{0,2},{1,3},{2,0},{3,1},{4,6},{5,7},{6,4},{7,5},{8,10},{9,11},{10,... | collective-permute-start | bytes 1376264 | tf_op jit(solution)/shard_map/ppermute | solution.py:523
  68.2 2.4 %collective-permute-start.6 = (bf16[256,640]{1,0:T(8,128)(2,1)}, bf16[256,640]{1,0:T(8,128)(2,1)S(1)}, u32[]{:S(2)}, u32[]{:S(2)}) collective-permute-start(bf16[256,640]{1,0:T(8,128)(2,1)} %collective-permute-done.2.refs_0_), channel_id=1, source_target_pairs={{0,1},{1,0},{2,3},{3,2},{4,5},{5,4},{6,7},{7,6},{8,9},{9,8},{10,11... | collective-permute-start | bytes 983048 | tf_op jit(solution)/shard_map/ppermute | solution.py:523
  70.6 4.0 %all-to-all-start.1 = ((bf16[32,16,512]{2,1,0:T(8,128)(2,1)}), bf16[32,16,512]{2,1,0:T(8,128)(2,1)S(1)}, u32[]{:S(2)}, u32[]{:S(2)}) async-start(bf16[32,16,512]{2,1,0:T(8,128)(2,1)} %bitcast.11), calls=%async_computation.1 | async-start | bytes 1048576 | tf_op jit(solution)/shard_map/all_to_all | solution.py:596
  75.2 4.2 %copy.18 = f32[64,64,128]{2,0,1:T(8,128)} copy(f32[64,64,128]{2,1,0:T(8,128)} %get-tuple-element.54) | data formatting | bytes 4194304 | tf_op jit(solution)/shard_map/optimization_barrier | solution.py:595
  80.7 4.8 %base.3.refs_9_ = f32[256,512]{1,0:T(8,128)} custom-call(s32[4]{0:T(128)} %pad_add_fusion.place_ref, bf16[256,640]{1,0:T(8,128)(2,1)} %collective-permute-done.2.refs_0_, bf16[256,640]{1,0:T(8,128)(2,1)} %copy-done.7, bf16[256,512]{1,0:T(8,128)(2,1)} %copy-done.8, bf16[256,512]{1,0:T(8,128)(2,1)} %copy-done.9, bf16[8192,256]{1,0:T(8,128)(2,1)} %refs_2_.3, ...), custom_call_target="tpu_custom_call" | custom-call | tf_op jit(solution)/shard_map/base/pallas_call | solution.py:278
  85.6 1.0 %collective-permute-start.9 = (bf16[256,896]{1,0:T(8,128)(2,1)S(1)}, bf16[256,896]{1,0:T(8,128)(2,1)S(1)}, u32[]{:S(2)}, u32[]{:S(2)}) collective-permute-start(bf16[256,896]{1,0:T(8,128)(2,1)S(1)} %collective-permute-done.8.refs_0_), channel_id=1, source_target_pairs={{0,1},{1,0},{2,3},{3,2},{4,5},{5,4},{6,7},{7,6},{8,9},{9,8},{10,11... | collective-permute-start | bytes 1376264 | tf_op jit(solution)/shard_map/ppermute | solution.py:523
  88.8 7.4 %final.1 = (bf16[4,64,2048]{2,1,0:T(8,128)(2,1)}, bf16[256,256]{1,0:T(8,128)(2,1)}, bf16[256,256]{1,0:T(8,128)(2,1)}) custom-call(s32[2]{0:T(128)} %get-tuple-element.75.place_ref, bf16[256,896]{1,0:T(8,128)(2,1)} %copy-done.5, bf16[256,896]{1,0:T(8,128)(2,1)} %copy-done.6, bf16[8192,256]{1,0:T(8,128)(2,1)} %refs_2_.3, bf16[8192,256]{1,0:T(8,128)(2,1)} %refs_3_.3, ...), custom_call_target="tpu_custom_call" | custom-call | flops 1000000000 | bytes 8388608 | tf_op jit(solution)/shard_map/final/pallas_call | solution.py:492
  (52 shorter events, 9.3 us)
Async XLA Ops:
  0.6 14.8 %copy-start.2 = (bf16[4,64,2048]{2,1,0:T(8,128)(2,1)S(1)}, bf16[4,64,2048]{2,1,0:T(8,128)(2,1)}, u32[]{:S(2)}) copy-start(bf16[4,64,2048]{2,1,0:T(8,128)(2,1)} %param.11) | copy-start | bytes 3145732
  4.1 15.2 %copy-start.10 = (s32[64]{0:T(128)S(1)}, s32[64]{0:T(128)}, u32[]{:S(2)}) copy-start(s32[64]{0:T(128)} %length_ref.1) | copy-start | bytes 772
  4.1 42.2 %all-to-all-start = ((bf16[32,16,2176]{2,1,0:T(8,128)(2,1)}), bf16[32,16,2176]{2,1,0:T(8,128)(2,1)S(1)}, u32[]{:S(2)}, u32[]{:S(2)}) async-start(bf16[32,16,2176]{2,1,0:T(8,128)(2,1)} %bitcast.34), calls=%async_computation | async-start | bytes 4456448 | tf_op jit(solution)/shard_map/all_to_all | solution.py:552
  15.4 19.6 %collective-permute-start = (bf16[256,2048]{1,0:T(8,128)(2,1)S(1)}, bf16[256,2048]{1,0:T(8,128)(2,1)}, u32[]{:S(2)}, u32[]{:S(2)}) collective-permute-start(bf16[256,2048]{1,0:T(8,128)(2,1)S(1)} %bitcast.29), channel_id=1, source_target_pairs={{0,1},{1,0},{2,3},{3,2},{4,5},{5,4},{6,7},{7,6},{8,9},{9,8},{10,11... | collective-permute-start | bytes 3145736 | tf_op jit(solution)/shard_map/ppermute | solution.py:523
  19.3 15.0 %copy-start.11 = (s32[4]{0:T(128)S(1)}, s32[4]{0:T(128)}, u32[]{:S(2)}) copy-start(s32[4]{0:T(128)} %param.20) | copy-start | bytes 52
  46.2 9.5 %collective-permute-start.2 = (bf16[256,640]{1,0:T(8,128)(2,1)}, bf16[256,640]{1,0:T(8,128)(2,1)}, u32[]{:S(2)}, u32[]{:S(2)}) collective-permute-start(bf16[256,640]{1,0:T(8,128)(2,1)} %slice.17), channel_id=1, source_target_pairs={{0,2},{1,3},{2,0},{3,1},{4,6},{5,7},{6,4},{7,5},{8,10},{9,11},{10,... | collective-permute-start | bytes 983048 | tf_op jit(solution)/shard_map/ppermute | solution.py:523
  46.6 2.2 %copy-start.1 = (bf16[4,2048,256]{2,1,0:T(8,128)(2,1)S(1)}, bf16[4,2048,256]{2,1,0:T(8,128)(2,1)}, u32[]{:S(2)}) copy-start(bf16[4,2048,256]{2,1,0:T(8,128)(2,1)} %weight_ref.2) | copy-start | bytes 12582916
  48.8 8.1 %copy-start.3 = (bf16[4,64,2048]{2,1,0:T(8,128)(2,1)S(1)}, bf16[4,64,2048]{2,1,0:T(8,128)(2,1)}, u32[]{:S(2)}) copy-start(bf16[4,64,2048]{2,1,0:T(8,128)(2,1)} %param.11) | copy-start | bytes 3145732
  48.8 15.4 %copy-start = (bf16[4,2,128,256]{3,2,1,0:T(8,128)(2,1)S(1)}, bf16[4,2,128,256]{3,2,1,0:T(8,128)(2,1)}, u32[]{:S(2)}) copy-start(bf16[4,2,128,256]{3,2,1,0:T(8,128)(2,1)} %weight_ref.3) | copy-start | bytes 1572868
  52.0 3.7 %collective-permute-start.1 = (f32[256,256]{1,0:T(8,128)S(1)}, f32[256,256]{1,0:T(8,128)S(1)}, u32[]{:S(2)}, u32[]{:S(2)}) collective-permute-start(f32[256,256]{1,0:T(8,128)S(1)} %get-tuple-element.45), channel_id=1, source_target_pairs={{0,1},{1,0},{2,3},{3,2},{4,5},{5,4},{6,7},{7,6},{8,9},{9,8},{10,11... | collective-permute-start | bytes 786440 | tf_op jit(solution)/shard_map/ppermute | solution.py:523
  55.7 3.9 %collective-permute-start.3 = (bf16[256,256]{1,0:T(8,128)(2,1)S(1)}, bf16[256,256]{1,0:T(8,128)(2,1)S(1)}, u32[]{:S(2)}, u32[]{:S(2)}) collective-permute-start(bf16[256,256]{1,0:T(8,128)(2,1)S(1)} %convert_element_type.25), channel_id=1, source_target_pairs={{0,2},{1,3},{2,0},{3,1},{4,6},{5,7},{6,4},{7,5},{8,10},{9,11},{10,... | collective-permute-start | bytes 393224 | tf_op jit(solution)/shard_map/ppermute | solution.py:523
  59.6 6.7 %collective-permute-start.5 = (bf16[256,512]{1,0:T(8,128)(2,1)S(1)}, bf16[256,512]{1,0:T(8,128)(2,1)S(1)}, u32[]{:S(2)}, u32[]{:S(2)}) collective-permute-start(bf16[256,512]{1,0:T(8,128)(2,1)S(1)} %slice.18), channel_id=1, source_target_pairs={{0,2},{1,3},{2,0},{3,1},{4,6},{5,7},{6,4},{7,5},{8,10},{9,11},{10,... | collective-permute-start | bytes 786440 | tf_op jit(solution)/shard_map/ppermute | solution.py:523
  61.6 2.5 %collective-permute-start.4 = (bf16[256,256]{1,0:T(8,128)(2,1)S(1)}, bf16[256,256]{1,0:T(8,128)(2,1)S(1)}, u32[]{:S(2)}, u32[]{:S(2)}) collective-permute-start(bf16[256,256]{1,0:T(8,128)(2,1)S(1)} %add_convert_fusion.own_ref), channel_id=1, source_target_pairs={{0,1},{1,0},{2,3},{3,2},{4,5},{5,4},{6,7},{7,6},{8,9},{9,8},{10,11... | collective-permute-start | bytes 393224 | tf_op jit(solution)/shard_map/ppermute | solution.py:523
  66.3 13.1 %copy-start.8 = (bf16[256,512]{1,0:T(8,128)(2,1)}, bf16[256,512]{1,0:T(8,128)(2,1)S(1)}, u32[]{:S(2)}) copy-start(bf16[256,512]{1,0:T(8,128)(2,1)S(1)} %collective-permute-done.5.refs_2_) | copy-start | bytes 786436
  66.3 19.3 %collective-permute-start.8 = (bf16[256,896]{1,0:T(8,128)(2,1)}, bf16[256,896]{1,0:T(8,128)(2,1)S(1)}, u32[]{:S(2)}, u32[]{:S(2)}) collective-permute-start(bf16[256,896]{1,0:T(8,128)(2,1)} %slice.19), channel_id=1, source_target_pairs={{0,2},{1,3},{2,0},{3,1},{4,6},{5,7},{6,4},{7,5},{8,10},{9,11},{10,... | collective-permute-start | bytes 1376264 | tf_op jit(solution)/shard_map/ppermute | solution.py:523
  68.2 11.2 %collective-permute-start.6 = (bf16[256,640]{1,0:T(8,128)(2,1)}, bf16[256,640]{1,0:T(8,128)(2,1)S(1)}, u32[]{:S(2)}, u32[]{:S(2)}) collective-permute-start(bf16[256,640]{1,0:T(8,128)(2,1)} %collective-permute-done.2.refs_0_), channel_id=1, source_target_pairs={{0,1},{1,0},{2,3},{3,2},{4,5},{5,4},{6,7},{7,6},{8,9},{9,8},{10,11... | collective-permute-start | bytes 983048 | tf_op jit(solution)/shard_map/ppermute | solution.py:523
  70.6 8.7 %collective-permute-start.7 = (bf16[256,512]{1,0:T(8,128)(2,1)S(1)}, bf16[256,512]{1,0:T(8,128)(2,1)S(1)}, u32[]{:S(2)}, u32[]{:S(2)}) collective-permute-start(bf16[256,512]{1,0:T(8,128)(2,1)S(1)} %collective-permute-done.5.refs_2_), channel_id=1, source_target_pairs={{0,1},{1,0},{2,3},{3,2},{4,5},{5,4},{6,7},{7,6},{8,9},{9,8},{10,11... | collective-permute-start | bytes 786440 | tf_op jit(solution)/shard_map/ppermute | solution.py:523
  70.6 16.7 %all-to-all-start.1 = ((bf16[32,16,512]{2,1,0:T(8,128)(2,1)}), bf16[32,16,512]{2,1,0:T(8,128)(2,1)S(1)}, u32[]{:S(2)}, u32[]{:S(2)}) async-start(bf16[32,16,512]{2,1,0:T(8,128)(2,1)} %bitcast.11), calls=%async_computation.1 | async-start | bytes 1048576 | tf_op jit(solution)/shard_map/all_to_all | solution.py:596
  79.3 0.7 copy-start.9
  80.0 0.7 copy-start.7
  85.6 2.5 %copy-start.5 = (bf16[256,896]{1,0:T(8,128)(2,1)}, bf16[256,896]{1,0:T(8,128)(2,1)S(1)}, u32[]{:S(2)}) copy-start(bf16[256,896]{1,0:T(8,128)(2,1)S(1)} %collective-permute-done.8.refs_0_) | copy-start | bytes 1376260
  85.6 2.5 %collective-permute-start.9 = (bf16[256,896]{1,0:T(8,128)(2,1)S(1)}, bf16[256,896]{1,0:T(8,128)(2,1)S(1)}, u32[]{:S(2)}, u32[]{:S(2)}) collective-permute-start(bf16[256,896]{1,0:T(8,128)(2,1)S(1)} %collective-permute-done.8.refs_0_), channel_id=1, source_target_pairs={{0,1},{1,0},{2,3},{3,2},{4,5},{5,4},{6,7},{7,6},{8,9},{9,8},{10,11... | collective-permute-start | bytes 1376264 | tf_op jit(solution)/shard_map/ppermute | solution.py:523
  87.3 0.8 copy-start.4
  88.1 0.8 copy-start.6

commit v4 on v3

--- a/solution.py
+++ b/solution.py
@@ -547,7 +547,7 @@
     odd = jnp.reshape(t % 2, (1,)).astype(jnp.int32)
 
     x = normed_input_rows.reshape(total, width)
-    cuts = (0, 5 * width // 16, 9 * width // 16, width)
+    cuts = (0, 5 * width // 16, 8 * width // 16, width)
     outgoing, sel = dispatch(adapter_index_rows, x, rows_dev, resident, replicas)
     landed = lax.all_to_all(outgoing, "rep", split_axis=0, concat_axis=0, tiled=True)
 

time: 97 us -> 107 us (1.10)
  blocking collectives: 0 us -> 18.6 us
  starting transfers between devices: 29.3 us -> 24.8 us
  local copies, waits for them, and re-layouts: 13 us -> 10.6 us
    all_to_all x0 -> x1, blocking collectives: none -> 18.6 us  [per_device(): lax.all_to_all(returned, 'rep', split_axis=0, concat_axis=0, tiled=True)]
    all_to_all x1 -> x0, starting transfers between devices: 3.98 us -> none  [per_device(): lax.all_to_all(returned, 'rep', split_axis=0, concat_axis=0, tiled=True)]
    optimization_barrier x1, local copies, waits for them, and re-layouts: 4.17 us -> 2.57 us  [per_device(): lax.optimization_barrier((returned, far0, far1, old, x_near[:, cuts[2]:]))]
    unnamed x25 -> x31, local copies, waits for them, and re-layouts: 5.84 us -> 5.88 us
  transfers between devices with their start and end apart: 12 -> 11, of which waited for: 7 -> 4; matrix products, arithmetic and copies ran while one was open for 12% -> 8% of each run, Pallas kernels for 30% -> 26%
where the time goes in v4:
time: 107 us
  Pallas kernels  38.8 us (36%)
  starting transfers between devices  24.8 us (23%)
  blocking collectives  18.6 us (17%)
  local copies, waits for them, and re-layouts  10.6 us (10%)
  waiting for transfers between devices  9.98 us (9%)
  other arithmetic  2.88 us (3%)
    all_to_all x1, blocking collectives, per_device(): lax.all_to_all(returned, 'rep', split_axis=0, concat_axis=0, tiled=True)  18.6 us
    ppermute x10, starting transfers between devices, swap(): return lax.ppermute(x, 'tp', [(i, i ^ bit) for i in range(count)])  13.5 us
    pallas_call x1, Pallas kernels, stored(): pl.pallas_call(functools.partial(stored_kernel, rows), grid_spec=pltpu.Pr...  12.7 us
    all_to_all x1, starting transfers between devices, per_device(): lax.all_to_all(outgoing, 'rep', split_axis=0, concat_axis=0, tiled=True)  11.4 us
    pallas_call x2, Pallas kernels, base(): pl.pallas_call(functools.partial(base_kernel, count, before is not None),...  11.2 us
    pallas_call x1, Pallas kernels, final(): pl.pallas_call(functools.partial(final_kernel, steps, count), in_specs=[p...  7.5 us
    unnamed x31, local copies, waits for them, and re-layouts  5.88 us
    ppermute x10, waiting for transfers between devices, swap(): return lax.ppermute(x, 'tp', [(i, i ^ bit) for i in range(count)])  5.21 us
  transfers between devices with their start and end apart: 11, of which 4 were waited for; matrix products, arithmetic and copies ran while one was open for 8% of the time, Pallas kernels for 26%

profile of v4, /device:TPU:1, one launch (start us, length us, event | category | flops | bytes accessed | tf_op | source)
XLA Modules:
  0.0 106.8 jit_solution(2772009804192537711)
XLA Ops:
  0.6 3.4 %dispatch.1 = (bf16[512,2176]{1,0:T(8,128)(2,1)}, bf16[256,512]{1,0:T(8,128)(2,1)}) custom-call(s32[4,64]{1,0:T(4,128)} %ids_hbm.1, bf16[256,2048]{1,0:T(8,128)(2,1)} %bitcast.28), custom_call_target="tpu_custom_call" | custom-call | flops 536870912 | bytes 3145728 | tf_op jit(solution)/shard_map/dispatch/pallas_call | solution.py:101
  4.0 11.4 %all-to-all-start = ((bf16[32,16,2176]{2,1,0:T(8,128)(2,1)}), bf16[32,16,2176]{2,1,0:T(8,128)(2,1)S(1)}, u32[]{:S(2)}, u32[]{:S(2)}) async-start(bf16[32,16,2176]{2,1,0:T(8,128)(2,1)} %bitcast.35), calls=%async_computation | async-start | bytes 4456448 | tf_op jit(solution)/shard_map/all_to_all | solution.py:552
  15.4 1.0 collective-permute-start
  16.4 1.4 %copy.16 = bf16[32,8,16,128]{3,2,1,0:T(8,128)(2,1)S(1)} copy(bf16[32,8,16,128]{3,1,2,0:T(8,128)(2,1)} %bitcast.34) | data formatting | bytes 2097152
  17.9 1.3 %copy.14 = bf16[4,64,2,8,128]{4,3,0,2,1:T(8,128)(2,1)} copy(bf16[4,64,2,8,128]{4,3,2,1,0:T(8,128)(2,1)S(1)} %bitcast.27) | data formatting | bytes 2097152 | tf_op jit(solution)/shard_map/reshape | solution.py:555
  19.3 12.7 %stored.1 = (f32[64,64,128]{2,1,0:T(8,128)}, f32[64,64]{1,0:T(8,128)}) custom-call(s32[64]{0:T(128)} %length_ref.1, bf16[64,64,128]{2,1,0:T(8,128)(2,1)} %bitcast.26, bf16[64,256,256]{2,1,0:T(8,128)(2,1)} %k_ref.1, bf16[64,256,256]{2,1,0:T(8,128)(2,1)} %v_ref.1), custom_call_target="tpu_custom_call" | custom-call | flops 536870912 | bytes 16777216 | tf_op jit(solution)/shard_map/stored/pallas_call | solution.py:340
  35.0 6.4 %base.2.refs_6_ = f32[256,512]{1,0:T(8,128)} custom-call(s32[2]{0:T(128)} %get-tuple-element.74.place_ref, bf16[256,2048]{1,0:T(8,128)(2,1)} %bitcast.29, bf16[256,2048]{1,0:T(8,128)(2,1)} %collective-permute-done.refs_1_, bf16[8192,256]{1,0:T(8,128)(2,1)} %refs_2_.3, bf16[8192,256]{1,0:T(8,128)(2,1)} %refs_3_.3), custom_call_target="tpu_custom_call" | custom-call | tf_op jit(solution)/shard_map/base/pallas_call | solution.py:278
  41.4 4.8 %all-to-all-done = bf16[32,16,2176]{2,1,0:T(8,128)(2,1)S(1)} async-done(((bf16[32,16,2176]{2,1,0:T(8,128)(2,1)}), bf16[32,16,2176]{2,1,0:T(8,128)(2,1)S(1)}, u32[]{:S(2)}, u32[]{:S(2)}) %all-to-all-start) | async-done | bytes 2228256 | tf_op jit(solution)/shard_map/all_to_all | solution.py:552
  46.6 2.2 %copy-done.1 = bf16[4,2048,256]{2,1,0:T(8,128)(2,1)S(1)} copy-done((bf16[4,2048,256]{2,1,0:T(8,128)(2,1)S(1)}, bf16[4,2048,256]{2,1,0:T(8,128)(2,1)}, u32[]{:S(2)}) %copy-start.1) | copy-done | bytes 4194328
  48.8 3.1 %down.1 = (f32[256,256]{1,0:T(8,128)S(1)}, f32[256,256]{1,0:T(8,128)S(1)}) custom-call(s32[1]{0:T(128)} %bitcast.4.odd_ref, bf16[512,2176]{1,0:T(8,128)(2,1)S(1)} %bitcast.22, bf16[4,2048,256]{2,1,0:T(8,128)(2,1)S(1)} %copy-done.1, f32[4,1,256]{2,1,0:T(1,128)S(1)} %reshape.69.factor_ref), custom_call_target="tpu_custom_call" | custom-call | flops 2147483648 | bytes 6422528 | tf_op jit(solution)/shard_map/down/pallas_call | solution.py:153
  52.0 2.5 %collective-permute-start.1 = (f32[256,256]{1,0:T(8,128)S(1)}, f32[256,256]{1,0:T(8,128)S(1)}, u32[]{:S(2)}, u32[]{:S(2)}) collective-permute-start(f32[256,256]{1,0:T(8,128)S(1)} %get-tuple-element.45), channel_id=1, source_target_pairs={{0,1},{1,0},{2,3},{3,2},{4,5},{5,4},{6,7},{7,6},{8,9},{9,8},{10,11... | collective-permute-start | bytes 786440 | tf_op jit(solution)/shard_map/ppermute | solution.py:523
  54.5 1.2 %collective-permute-done.1 = f32[256,256]{1,0:T(8,128)S(1)} collective-permute-done((f32[256,256]{1,0:T(8,128)S(1)}, f32[256,256]{1,0:T(8,128)S(1)}, u32[]{:S(2)}, u32[]{:S(2)}) %collective-permute-start.1) | collective-permute-done | bytes 262176 | tf_op jit(solution)/shard_map/ppermute | solution.py:523
  55.7 1.1 %collective-permute-start.3 = (bf16[256,256]{1,0:T(8,128)(2,1)S(1)}, bf16[256,256]{1,0:T(8,128)(2,1)S(1)}, u32[]{:S(2)}, u32[]{:S(2)}) collective-permute-start(bf16[256,256]{1,0:T(8,128)(2,1)S(1)} %convert_element_type.25), channel_id=1, source_target_pairs={{0,2},{1,3},{2,0},{3,1},{4,6},{5,7},{6,4},{7,5},{8,10},{9,11},{10,... | collective-permute-start | bytes 393224 | tf_op jit(solution)/shard_map/ppermute | solution.py:523
  56.9 3.1 %collective-permute-done.3 = bf16[256,256]{1,0:T(8,128)(2,1)S(1)} collective-permute-done((bf16[256,256]{1,0:T(8,128)(2,1)S(1)}, bf16[256,256]{1,0:T(8,128)(2,1)S(1)}, u32[]{:S(2)}, u32[]{:S(2)}) %collective-permute-start.3) | collective-permute-done | bytes 131104 | tf_op jit(solution)/shard_map/ppermute | solution.py:523
  60.0 1.6 %collective-permute-start.5 = (bf16[256,384]{1,0:T(8,128)(2,1)S(1)}, bf16[256,384]{1,0:T(8,128)(2,1)S(1)}, u32[]{:S(2)}, u32[]{:S(2)}) collective-permute-start(bf16[256,384]{1,0:T(8,128)(2,1)S(1)} %slice.18), channel_id=1, source_target_pairs={{0,2},{1,3},{2,0},{3,1},{4,6},{5,7},{6,4},{7,5},{8,10},{9,11},{10,... | collective-permute-start | bytes 589832 | tf_op jit(solution)/shard_map/ppermute | solution.py:523
  61.6 1.6 %collective-permute-start.4 = (bf16[256,256]{1,0:T(8,128)(2,1)S(1)}, bf16[256,256]{1,0:T(8,128)(2,1)S(1)}, u32[]{:S(2)}, u32[]{:S(2)}) collective-permute-start(bf16[256,256]{1,0:T(8,128)(2,1)S(1)} %add_convert_fusion.own_ref), channel_id=1, source_target_pairs={{0,1},{1,0},{2,3},{3,2},{4,5},{5,4},{6,7},{7,6},{8,9},{9,8},{10,11... | collective-permute-start | bytes 393224 | tf_op jit(solution)/shard_map/ppermute | solution.py:523
  63.2 0.9 collective-permute-done.4.other_ref
  65.0 1.8 %collective-permute-start.8 = (bf16[256,1024]{1,0:T(8,128)(2,1)S(1)}, bf16[256,1024]{1,0:T(8,128)(2,1)S(1)}, u32[]{:S(2)}, u32[]{:S(2)}) collective-permute-start(bf16[256,1024]{1,0:T(8,128)(2,1)S(1)} %slice.19), channel_id=1, source_target_pairs={{0,2},{1,3},{2,0},{3,1},{4,6},{5,7},{6,4},{7,5},{8,10},{9,11},{10,... | collective-permute-start | bytes 1572872 | tf_op jit(solution)/shard_map/ppermute | solution.py:523
  66.8 2.4 %collective-permute-start.6 = (bf16[256,640]{1,0:T(8,128)(2,1)S(1)}, bf16[256,640]{1,0:T(8,128)(2,1)S(1)}, u32[]{:S(2)}, u32[]{:S(2)}) collective-permute-start(bf16[256,640]{1,0:T(8,128)(2,1)S(1)} %collective-permute-done.2.refs_0_), channel_id=1, source_target_pairs={{0,1},{1,0},{2,3},{3,2},{4,5},{5,4},{6,7},{7,6},{8,9},{9,8},{10,11... | collective-permute-start | bytes 983048 | tf_op jit(solution)/shard_map/ppermute | solution.py:523
  69.8 2.6 %copy.18 = f32[64,64,128]{2,0,1:T(8,128)} copy(f32[64,64,128]{2,1,0:T(8,128)S(1)} %copy-done.4) | data formatting | bytes 4194304 | tf_op jit(solution)/shard_map/optimization_barrier | solution.py:595
  73.8 4.8 %base.3.refs_9_ = f32[256,512]{1,0:T(8,128)} custom-call(s32[4]{0:T(128)} %pad_add_fusion.place_ref, bf16[256,640]{1,0:T(8,128)(2,1)} %copy-done.7, bf16[256,640]{1,0:T(8,128)(2,1)} %copy-done.8, bf16[256,384]{1,0:T(8,128)(2,1)} %copy-done.9, bf16[256,384]{1,0:T(8,128)(2,1)} %copy-done.10, bf16[8192,256]{1,0:T(8,128)(2,1)} %refs_2_.3, ...), custom_call_target="tpu_custom_call" | custom-call | tf_op jit(solution)/shard_map/base/pallas_call | solution.py:278
  78.6 1.1 collective-permute-start.9
  79.7 18.6 %all_to_all.24 = bf16[32,16,512]{2,1,0:T(8,128)(2,1)} all-to-all(bf16[32,16,512]{2,1,0:T(8,128)(2,1)S(1)} %bitcast.24), channel_id=1, replica_groups=mesh['rep'=32,'tp'=4] {'rep'}, dimensions={0} | all-to-all | bytes 1048576 | tf_op jit(solution)/shard_map/all_to_all | solution.py:596
  99.1 7.5 %final.1 = (bf16[4,64,2048]{2,1,0:T(8,128)(2,1)}, bf16[256,256]{1,0:T(8,128)(2,1)}, bf16[256,256]{1,0:T(8,128)(2,1)}) custom-call(s32[2]{0:T(128)} %get-tuple-element.75.place_ref, bf16[256,1024]{1,0:T(8,128)(2,1)} %copy-done.5, bf16[256,1024]{1,0:T(8,128)(2,1)} %copy-done.6, bf16[8192,256]{1,0:T(8,128)(2,1)} %refs_2_.3, bf16[8192,256]{1,0:T(8,128)(2,1)} %refs_3_.3, ...), custom_call_target="tpu_custom_call" | custom-call | flops 1000000000 | bytes 8388608 | tf_op jit(solution)/shard_map/final/pallas_call | solution.py:492
  (57 shorter events, 7.2 us)
Async XLA Ops:
  0.6 14.8 %copy-start.2 = (bf16[4,64,2048]{2,1,0:T(8,128)(2,1)S(1)}, bf16[4,64,2048]{2,1,0:T(8,128)(2,1)}, u32[]{:S(2)}) copy-start(bf16[4,64,2048]{2,1,0:T(8,128)(2,1)} %param.11) | copy-start | bytes 3145732
  4.0 15.2 %copy-start.11 = (s32[64]{0:T(128)S(1)}, s32[64]{0:T(128)}, u32[]{:S(2)}) copy-start(s32[64]{0:T(128)} %length_ref.1) | copy-start | bytes 772
  4.0 42.2 %all-to-all-start = ((bf16[32,16,2176]{2,1,0:T(8,128)(2,1)}), bf16[32,16,2176]{2,1,0:T(8,128)(2,1)S(1)}, u32[]{:S(2)}, u32[]{:S(2)}) async-start(bf16[32,16,2176]{2,1,0:T(8,128)(2,1)} %bitcast.35), calls=%async_computation | async-start | bytes 4456448 | tf_op jit(solution)/shard_map/all_to_all | solution.py:552
  15.4 19.6 %collective-permute-start = (bf16[256,2048]{1,0:T(8,128)(2,1)S(1)}, bf16[256,2048]{1,0:T(8,128)(2,1)}, u32[]{:S(2)}, u32[]{:S(2)}) collective-permute-start(bf16[256,2048]{1,0:T(8,128)(2,1)S(1)} %bitcast.30), channel_id=1, source_target_pairs={{0,1},{1,0},{2,3},{3,2},{4,5},{5,4},{6,7},{7,6},{8,9},{9,8},{10,11... | collective-permute-start | bytes 3145736 | tf_op jit(solution)/shard_map/ppermute | solution.py:523
  19.3 15.0 %copy-start.12 = (s32[4]{0:T(128)S(1)}, s32[4]{0:T(128)}, u32[]{:S(2)}) copy-start(s32[4]{0:T(128)} %param.20) | copy-start | bytes 52
  46.2 9.5 %collective-permute-start.2 = (bf16[256,640]{1,0:T(8,128)(2,1)}, bf16[256,640]{1,0:T(8,128)(2,1)S(1)}, u32[]{:S(2)}, u32[]{:S(2)}) collective-permute-start(bf16[256,640]{1,0:T(8,128)(2,1)} %slice.17), channel_id=1, source_target_pairs={{0,2},{1,3},{2,0},{3,1},{4,6},{5,7},{6,4},{7,5},{8,10},{9,11},{10,... | collective-permute-start | bytes 983048 | tf_op jit(solution)/shard_map/ppermute | solution.py:523
  46.6 2.2 %copy-start.1 = (bf16[4,2048,256]{2,1,0:T(8,128)(2,1)S(1)}, bf16[4,2048,256]{2,1,0:T(8,128)(2,1)}, u32[]{:S(2)}) copy-start(bf16[4,2048,256]{2,1,0:T(8,128)(2,1)} %weight_ref.2) | copy-start | bytes 12582916
  48.8 8.1 %copy-start.3 = (bf16[4,64,2048]{2,1,0:T(8,128)(2,1)S(1)}, bf16[4,64,2048]{2,1,0:T(8,128)(2,1)}, u32[]{:S(2)}) copy-start(bf16[4,64,2048]{2,1,0:T(8,128)(2,1)} %param.11) | copy-start | bytes 3145732
  48.8 15.4 %copy-start = (bf16[4,2,128,256]{3,2,1,0:T(8,128)(2,1)S(1)}, bf16[4,2,128,256]{3,2,1,0:T(8,128)(2,1)}, u32[]{:S(2)}) copy-start(bf16[4,2,128,256]{3,2,1,0:T(8,128)(2,1)} %weight_ref.3) | copy-start | bytes 1572868
  51.9 17.3 %copy-start.13 = (s32[2]{0:T(128)S(1)}, s32[2]{0:T(128)}, u32[]{:S(2)}) copy-start(s32[2]{0:T(128)} %get-tuple-element.76) | copy-start | bytes 28
  52.0 17.3 %copy-start.14 = (s32[2]{0:T(128)S(1)}, s32[2]{0:T(128)}, u32[]{:S(2)}) copy-start(s32[2]{0:T(128)} %get-tuple-element.77) | copy-start | bytes 28
  52.0 17.8 %copy-start.4 = (f32[64,64,128]{2,1,0:T(8,128)S(1)}, f32[64,64,128]{2,1,0:T(8,128)}, u32[]{:S(2)}) copy-start(f32[64,64,128]{2,1,0:T(8,128)} %get-tuple-element.54) | copy-start | bytes 6291460
  52.0 3.7 %collective-permute-start.1 = (f32[256,256]{1,0:T(8,128)S(1)}, f32[256,256]{1,0:T(8,128)S(1)}, u32[]{:S(2)}, u32[]{:S(2)}) collective-permute-start(f32[256,256]{1,0:T(8,128)S(1)} %get-tuple-element.45), channel_id=1, source_target_pairs={{0,1},{1,0},{2,3},{3,2},{4,5},{5,4},{6,7},{7,6},{8,9},{9,8},{10,11... | collective-permute-start | bytes 786440 | tf_op jit(solution)/shard_map/ppermute | solution.py:523
  55.7 16.7 %copy-start.7 = (bf16[256,640]{1,0:T(8,128)(2,1)}, bf16[256,640]{1,0:T(8,128)(2,1)S(1)}, u32[]{:S(2)}) copy-start(bf16[256,640]{1,0:T(8,128)(2,1)S(1)} %collective-permute-done.2.refs_0_) | copy-start | bytes 983044
  55.7 4.3 %collective-permute-start.3 = (bf16[256,256]{1,0:T(8,128)(2,1)S(1)}, bf16[256,256]{1,0:T(8,128)(2,1)S(1)}, u32[]{:S(2)}, u32[]{:S(2)}) collective-permute-start(bf16[256,256]{1,0:T(8,128)(2,1)S(1)} %convert_element_type.25), channel_id=1, source_target_pairs={{0,2},{1,3},{2,0},{3,1},{4,6},{5,7},{6,4},{7,5},{8,10},{9,11},{10,... | collective-permute-start | bytes 393224 | tf_op jit(solution)/shard_map/ppermute | solution.py:523
  60.0 5.0 %collective-permute-start.5 = (bf16[256,384]{1,0:T(8,128)(2,1)S(1)}, bf16[256,384]{1,0:T(8,128)(2,1)S(1)}, u32[]{:S(2)}, u32[]{:S(2)}) collective-permute-start(bf16[256,384]{1,0:T(8,128)(2,1)S(1)} %slice.18), channel_id=1, source_target_pairs={{0,2},{1,3},{2,0},{3,1},{4,6},{5,7},{6,4},{7,5},{8,10},{9,11},{10,... | collective-permute-start | bytes 589832 | tf_op jit(solution)/shard_map/ppermute | solution.py:523
  61.6 2.5 %collective-permute-start.4 = (bf16[256,256]{1,0:T(8,128)(2,1)S(1)}, bf16[256,256]{1,0:T(8,128)(2,1)S(1)}, u32[]{:S(2)}, u32[]{:S(2)}) collective-permute-start(bf16[256,256]{1,0:T(8,128)(2,1)S(1)} %add_convert_fusion.own_ref), channel_id=1, source_target_pairs={{0,1},{1,0},{2,3},{3,2},{4,5},{5,4},{6,7},{7,6},{8,9},{9,8},{10,11... | collective-permute-start | bytes 393224 | tf_op jit(solution)/shard_map/ppermute | solution.py:523
  65.0 7.4 %copy-start.9 = (bf16[256,384]{1,0:T(8,128)(2,1)}, bf16[256,384]{1,0:T(8,128)(2,1)S(1)}, u32[]{:S(2)}) copy-start(bf16[256,384]{1,0:T(8,128)(2,1)S(1)} %collective-permute-done.5.refs_2_) | copy-start | bytes 589828
  65.0 13.6 %collective-permute-start.8 = (bf16[256,1024]{1,0:T(8,128)(2,1)S(1)}, bf16[256,1024]{1,0:T(8,128)(2,1)S(1)}, u32[]{:S(2)}, u32[]{:S(2)}) collective-permute-start(bf16[256,1024]{1,0:T(8,128)(2,1)S(1)} %slice.19), channel_id=1, source_target_pairs={{0,2},{1,3},{2,0},{3,1},{4,6},{5,7},{6,4},{7,5},{8,10},{9,11},{10,... | collective-permute-start | bytes 1572872 | tf_op jit(solution)/shard_map/ppermute | solution.py:523
  66.8 5.6 %collective-permute-start.6 = (bf16[256,640]{1,0:T(8,128)(2,1)S(1)}, bf16[256,640]{1,0:T(8,128)(2,1)S(1)}, u32[]{:S(2)}, u32[]{:S(2)}) collective-permute-start(bf16[256,640]{1,0:T(8,128)(2,1)S(1)} %collective-permute-done.2.refs_0_), channel_id=1, source_target_pairs={{0,1},{1,0},{2,3},{3,2},{4,5},{5,4},{6,7},{7,6},{8,9},{9,8},{10,11... | collective-permute-start | bytes 983048 | tf_op jit(solution)/shard_map/ppermute | solution.py:523
  69.2 3.2 %collective-permute-start.7 = (bf16[256,384]{1,0:T(8,128)(2,1)S(1)}, bf16[256,384]{1,0:T(8,128)(2,1)S(1)}, u32[]{:S(2)}, u32[]{:S(2)}) collective-permute-start(bf16[256,384]{1,0:T(8,128)(2,1)S(1)} %collective-permute-done.5.refs_2_), channel_id=1, source_target_pairs={{0,1},{1,0},{2,3},{3,2},{4,5},{5,4},{6,7},{7,6},{8,9},{9,8},{10,11... | collective-permute-start | bytes 589832 | tf_op jit(solution)/shard_map/ppermute | solution.py:523
  78.6 19.7 %copy-start.5 = (bf16[256,1024]{1,0:T(8,128)(2,1)}, bf16[256,1024]{1,0:T(8,128)(2,1)S(1)}, u32[]{:S(2)}) copy-start(bf16[256,1024]{1,0:T(8,128)(2,1)S(1)} %collective-permute-done.8.refs_0_) | copy-start | bytes 1572868
  78.6 19.7 %collective-permute-start.9 = (bf16[256,1024]{1,0:T(8,128)(2,1)S(1)}, bf16[256,1024]{1,0:T(8,128)(2,1)S(1)}, u32[]{:S(2)}, u32[]{:S(2)}) collective-permute-start(bf16[256,1024]{1,0:T(8,128)(2,1)S(1)} %collective-permute-done.8.refs_0_), channel_id=1, source_target_pairs={{0,1},{1,0},{2,3},{3,2},{4,5},{5,4},{6,7},{7,6},{8,9},{9,8},{10,11... | collective-permute-start | bytes 1572872 | tf_op jit(solution)/shard_map/ppermute | solution.py:523
  98.3 0.8 copy-start.6
  (2 other events, 1.4 us)
